TPU v7x, 1024 devices: a whole 8x8x8 slice. The times are simulated.
1024 devices in a mesh: fsdp: 64 (over y, x), tensor: 16 (over z, core).
Axes of the slice: x: 8, y: 8, z: 8, core: 2. Of those that a mesh axis runs over, the one named last changes fastest.
Arguments:
- weight: float32 [4096, 14336], P('fsdp', 'tensor'), may hold values from -6 to 6
- momentum: float32 [4096, 14336], P('fsdp', 'tensor'), may hold values from -6 to 6
- gradient: bfloat16 [4096, 14336], P('fsdp', 'tensor'), may hold values from -90 to 90, as said below
- right_basis: float32 [14336, 64], P('tensor'), may hold values from -0.046875 to 0.046875
Outputs:
- new_weight: float32 [4096, 14336], P('fsdp', 'tensor')
- new_momentum: float32 [4096, 14336], P('fsdp', 'tensor')
- new_basis: float32 [14336, 64], P('tensor')
Inputs may be any that keep to these rules, and one draw needn't show every extreme that they name: Entries of the gradient are real-valued with row and column scales that differ widely.
All inputs are finite; a program needn't handle non-finite values.
Results may differ from a plain program's by a relative error of at most 0.0004.
Values sent between devices are 32-bit elements; how exact they have to be, the bound alone decides.
No kernel may reach another device: no remote copies, remote signals or barrier semaphores. Data moves between devices by JAX's collectives and lax.ppermute only.
A program may use at most 32 MiB of HBM per device.

v0:
```python
import math

import jax
import jax.numpy as jnp
from jax import lax
from jax.sharding import PartitionSpec as P

decay_rate = 0.95
step_size = 0.3
tiny_eps = 1e-08


def per_device(weight, momentum, gradient, right_basis):
    highest = lax.Precision.HIGHEST
    buffer = momentum + gradient.astype(jnp.float32)
    left_part = jnp.dot(buffer, right_basis, precision=highest)
    left = lax.psum(left_part, "tensor")
    gram_part = jnp.dot(left.T, left, precision=highest)
    gram_matrix = lax.psum(gram_part, "fsdp")
    lower_factor = jnp.linalg.cholesky(gram_matrix)
    ortho = jax.scipy.linalg.solve_triangular(lower_factor, left.T, lower=True).T
    right_part = jnp.dot(buffer.T, ortho, precision=highest)
    right_factor = lax.psum(right_part, "fsdp")
    square_sums = lax.psum(jnp.sum(right_factor * right_factor, axis=0), "tensor")
    norms = jnp.sqrt(square_sums)
    new_basis = right_factor / (norms + tiny_eps)
    new_momentum = buffer - (1.0 - decay_rate) * jnp.dot(ortho, right_factor.T, precision=highest)
    total_rows = weight.shape[0] * lax.axis_size("fsdp")
    total_cols = weight.shape[1] * lax.axis_size("tensor")
    factor = step_size * math.sqrt(total_rows * total_cols / right_basis.shape[1])
    new_weight = weight - factor * jnp.dot(ortho, new_basis.T, precision=highest)
    return (new_weight, new_momentum, new_basis)


def solution(mesh):
    placed = (P("fsdp", "tensor"), P("fsdp", "tensor"), P("fsdp", "tensor"), P("tensor", None))
    return jax.shard_map(
        per_device,
        mesh=mesh,
        in_specs=placed,
        out_specs=(P("fsdp", "tensor"), P("fsdp", "tensor"), P("tensor", None)),
        check_vma=False,
    )
```

profile of v0, /device:TPU:1, one launch (start us, length us, event | category | flops | bytes accessed | tf_op | source)
XLA Modules:
  0.0 552.9 jit_solution(5187902011087983940)
XLA Ops:
  7.2 0.0 copy-start
  7.2 0.0 all-reduce.2.cloned.1.call-start
  7.2 0.9 copy-done
  8.1 1.4 fusion.3
  9.5 58.4 %psum.28 = f32[64,64]{1,0:T(8,128)S(1)} all-reduce(f32[64,64]{1,0:T(8,128)S(1)} %fusion.3), channel_id=1, replica_groups=mesh['fsdp'=64,'tensor'=16] {'tensor'}, use_global_device_ids=true, to_apply=%region_0.0 | all-reduce | flops 4096 | bytes 32768 | tf_op jit(solution)/shard_map/psum | solution.py:17
  67.9 0.2 fusion.8
  68.1 0.0 copy-start.2
  68.1 225.8 %psum.29 = f32[64,64]{0,1:T(8,128)S(1)} all-reduce(f32[64,64]{0,1:T(8,128)S(1)} %fusion.8), channel_id=1, replica_groups=mesh['fsdp'=64,'tensor'=16] {'fsdp'}, use_global_device_ids=true, to_apply=%region_1.0 | all-reduce | flops 4096 | bytes 32768 | tf_op jit(solution)/shard_map/psum | solution.py:19
  293.9 0.1 copy.8
  294.0 0.0 copy-start.3
  294.0 5.8 %cholesky.16 = f32[64,64]{1,0:T(8,128)S(1)} custom-call(f32[64,64]{1,0:T(8,128)S(1)} %fusion.7), custom_call_target="Cholesky" | custom-call | tf_op jit(solution)/shard_map/jit(cholesky)/cholesky | solution.py:20
  299.9 0.6 compare_reduce_fusion
  300.5 0.7 fusion.4
  301.2 4.9 custom-call.7
  306.1 0.2 fusion.5
  306.3 0.0 copy-done.2
  306.3 0.0 copy-done.3
  306.3 1.0 fusion.2
  307.4 0.0 all-reduce.2.cloned.1.call-update
  307.4 204.7 %all-reduce.2.cloned.1.call-done = f32[896,64]{0,1:T(8,128)} async-done(((f32[896,64]{0,1:T(8,128)}), f32[896,64]{0,1:T(8,128)}) %all-reduce.2.cloned.1.call-update) | async-done | bytes 229392 | tf_op jit(solution)/shard_map/psum | solution.py:23
  512.1 0.0 copy-start.1
  512.1 1.1 multiply_reduce_fusion
  513.2 29.7 %psum.31 = f32[64]{0:T(128)S(1)} all-reduce(f32[64]{0:T(128)S(1)} %multiply_reduce_fusion), channel_id=1, replica_groups=mesh['fsdp'=64,'tensor'=16] {'tensor'}, use_global_device_ids=true, to_apply=%region_6.7 | all-reduce | flops 64 | bytes 512 | tf_op jit(solution)/shard_map/psum | solution.py:24
  542.9 0.0 copy-done.1
  542.9 0.0 copy-start.5
  542.9 0.1 broadcast_divide_fusion
  543.0 0.8 copy-done.5
  543.8 0.0 copy-start.4
  543.9 1.1 fusion.1
  544.9 0.0 copy-done.4
  544.9 1.1 fusion
  (3 shorter events, 0.0 us)
Async XLA Ops:
  7.2 0.9 copy-start
  7.2 504.9 %all-reduce.2.cloned.1.call-start = ((), (), s32[]{:S(2)}) async-start(), calls=%async_computation | async-start | bytes 458752 | tf_op jit(solution)/shard_map/psum | solution.py:23
  68.1 238.2 %copy-start.2 = (f32[64,896]{1,0:T(8,128)S(1)}, f32[64,896]{1,0:T(8,128)}, u32[]{:S(2)}) copy-start(f32[64,896]{1,0:T(8,128)} %param.5) | copy-start | bytes 688132
  294.0 12.4 %copy-start.3 = (bf16[64,896]{1,0:T(8,128)(2,1)S(1)}, bf16[64,896]{1,0:T(8,128)(2,1)}, u32[]{:S(2)}) copy-start(bf16[64,896]{1,0:T(8,128)(2,1)} %param.6) | copy-start | bytes 344068
  512.1 30.8 %copy-start.1 = (f32[896,64]{0,1:T(8,128)S(1)}, f32[896,64]{0,1:T(8,128)}, u32[]{:S(2)}) copy-start(f32[896,64]{0,1:T(8,128)} %all-reduce.2.cloned.1.call-done) | copy-start | bytes 688132
  542.9 0.9 copy-start.5
  543.8 1.1 copy-start.4
Sparse Core Ops, SparseCore 0:
  307.5 204.5 all-reduce.1
where the time goes:
time: 553 us
  blocking collectives  314 us (57%)
  waiting for transfers between devices  205 us (37%)
  between operations  14.1 us (3%)
  other arithmetic  13.3 us (2%)
    psum x1, blocking collectives, per_device(): gram_matrix = lax.psum(gram_part, 'fsdp')  226 us
    psum x1, waiting for transfers between devices, per_device(): right_factor = lax.psum(right_part, 'fsdp')  205 us
    psum x1, blocking collectives, per_device(): left = lax.psum(left_part, 'tensor')  58.4 us
    psum x1, blocking collectives, per_device(): lax.psum(jnp.sum(right_factor * right_factor, axis=0), 'tensor')  29.7 us
  transfers between devices with their start and end apart: 1, of which 1 were waited for; matrix products, arithmetic and copies ran while one was open for 0% of the time, Pallas kernels for 0%

commit v1 on v0

v1 whole, which is shorter than its diff:
```python
import math

import jax
import jax.numpy as jnp
from jax import lax
from jax.sharding import PartitionSpec as P

decay_rate = 0.95
step_size = 0.3
tiny_eps = 1e-08


def exchange(blocks, axis):
    return lax.all_to_all(blocks, axis, 0, 0)


def sum_everywhere(block, axis):
    copies = jnp.broadcast_to(block[None], (lax.axis_size(axis),) + block.shape)
    return jnp.sum(exchange(copies, axis), axis=0)


def gather(block, axis):
    copies = jnp.broadcast_to(block[None], (lax.axis_size(axis),) + block.shape)
    return exchange(copies, axis)


def per_device(weight, momentum, gradient, right_basis):
    highest = lax.Precision.HIGHEST
    rank = right_basis.shape[1]
    rows, cols = weight.shape
    buffer = momentum + gradient.astype(jnp.float32)
    left_part = jnp.dot(buffer, right_basis, precision=highest)
    half = rows // 2
    packed = jnp.concatenate([left_part[:half], left_part[half:]], axis=1)
    packed = sum_everywhere(packed, "tensor")
    left = jnp.concatenate([packed[:, :rank], packed[:, rank:]], axis=0)
    wide = jnp.concatenate([buffer, left, jnp.zeros((rows, 1024 - cols - rank), jnp.float32)], axis=1)
    products = jnp.dot(left.T, wide, precision=highest).reshape(rank, 8, 128)
    mine = jnp.sum(exchange(products, "fsdp"), axis=0)
    whole = gather(mine, "fsdp").reshape(rank, 1024)
    gram_matrix = whole[:, cols:cols + rank]
    lower_factor = jnp.linalg.cholesky(gram_matrix)
    both = jnp.concatenate([whole[:, :cols], left.T], axis=1)
    both = jax.scipy.linalg.solve_triangular(lower_factor, both, lower=True)
    right_t = both[:, :cols]
    ortho = both[:, cols:].T
    right_factor = right_t.T
    squares = jnp.sum(right_factor * right_factor, axis=0)
    squares = jnp.broadcast_to(jnp.pad(squares, (0, 128 - rank))[None], (8, 128))
    norms = jnp.sqrt(sum_everywhere(squares, "tensor")[0, :rank])
    new_basis = right_factor / (norms + tiny_eps)
    new_momentum = buffer - (1.0 - decay_rate) * jnp.dot(ortho, right_t, precision=highest)
    total_rows = weight.shape[0] * lax.axis_size("fsdp")
    total_cols = weight.shape[1] * lax.axis_size("tensor")
    factor = step_size * math.sqrt(total_rows * total_cols / rank)
    new_weight = weight - factor * jnp.dot(ortho, new_basis.T, precision=highest)
    return (new_weight, new_momentum, new_basis)


def solution(mesh):
    placed = (P("fsdp", "tensor"), P("fsdp", "tensor"), P("fsdp", "tensor"), P("tensor", None))
    return jax.shard_map(
        per_device,
        mesh=mesh,
        in_specs=placed,
        out_specs=(P("fsdp", "tensor"), P("fsdp", "tensor"), P("tensor", None)),
        check_vma=False,
    )
```

time: 553 us -> 109 us (0.20)
  blocking collectives: 314 us -> 56.7 us
  waiting for transfers between devices: 205 us -> 19.3 us
  between operations: 14.1 us -> 0.77 us
  starting transfers between devices: 0.04 us -> 11.5 us
    psum x3 -> x0, blocking collectives: 314 us -> none  [the longest x1 226 us: per_device(): gram_matrix = lax.psum(gram_part, 'fsdp')]
    psum x1 -> x0, waiting for transfers between devices: 205 us -> none  [per_device(): right_factor = lax.psum(right_part, 'fsdp')]
    all_to_all x0 -> x2, blocking collectives: none -> 56.7 us  [exchange(): return lax.all_to_all(blocks, axis, 0, 0)]
    all_to_all x0 -> x2, waiting for transfers between devices: none -> 19.3 us  [exchange(): return lax.all_to_all(blocks, axis, 0, 0)]
    all_to_all x0 -> x2, starting transfers between devices: none -> 11.5 us  [exchange(): return lax.all_to_all(blocks, axis, 0, 0)]
  transfers between devices with their start and end apart: 1 -> 2, of which waited for: 1 -> 2; matrix products, arithmetic and copies ran while one was open for 0% -> 1% of each run, Pallas kernels for 0% -> 0%
where the time goes in v1:
time: 109 us; the launch traced here: 108 us
  blocking collectives  56.7 us (52%)
  waiting for transfers between devices  19.3 us (18%)
  other arithmetic  14.2 us (13%)
  starting transfers between devices  11.5 us (11%)
  matrix products  3.69 us (3%)
  local copies, waits for them, and re-layouts  2.02 us (2%)
    all_to_all x2, blocking collectives, exchange(): return lax.all_to_all(blocks, axis, 0, 0)  56.7 us
    all_to_all x2, waiting for transfers between devices, exchange(): return lax.all_to_all(blocks, axis, 0, 0)  19.3 us
    all_to_all x2, starting transfers between devices, exchange(): return lax.all_to_all(blocks, axis, 0, 0)  11.5 us
    another operation x3, other arithmetic, per_device(): lower_factor = jnp.linalg.cholesky(gram_matrix)  6.52 us
    another operation x2, other arithmetic, per_device(): both = jax.scipy.linalg.solve_triangular(lower_factor, both, lower=True)  5.55 us
  transfers between devices with their start and end apart: 2, of which 2 were waited for; matrix products, arithmetic and copies ran while one was open for 1% of the time, Pallas kernels for 0%

profile of v1, /device:TPU:1, one launch (start us, length us, event | category | flops | bytes accessed | tf_op | source)
XLA Modules:
  0.0 108.2 jit_solution(5437962847670012480)
XLA Ops:
  0.6 0.0 copy-start
  0.6 1.1 convert_add_fusion
  1.7 0.0 copy-done
  1.7 0.4 fusion.25
  2.1 0.1 pad_maximum_fusion.2
  2.2 29.7 %all_to_all.20 = f32[16,32,128]{2,1,0:T(8,128)S(1)} all-to-all(f32[16,32,128]{2,1,0:T(8,128)S(1)} %broadcast_in_dim.7), channel_id=1, replica_groups=mesh['fsdp'=64,'tensor'=16] {'tensor'}, dimensions={0} | all-to-all | bytes 524288 | tf_op jit(solution)/shard_map/all_to_all | solution.py:14
  31.9 0.1 fusion.24
  32.0 0.4 convolution_bitcast_fusion
  32.5 27.0 %all_to_all.21 = f32[64,8,128]{2,1,0:T(8,128)S(1)} all-to-all(f32[64,8,128]{2,1,0:T(8,128)S(1)} %bitcast.24), channel_id=1, replica_groups=mesh['fsdp'=64,'tensor'=16] {'fsdp'}, dimensions={0} | all-to-all | bytes 524288 | tf_op jit(solution)/shard_map/all_to_all | solution.py:14
  59.5 0.1 reduce_sum.37
  59.6 0.7 broadcast_in_dim.9
  60.3 4.9 %all-to-all-start.2 = ((f32[64,8,128]{2,1,0:T(8,128)}), f32[64,8,128]{2,1,0:T(8,128)S(1)}, u32[]{:S(2)}, u32[]{:S(2)}) async-start(f32[64,8,128]{2,1,0:T(8,128)} %broadcast_in_dim.9), calls=%async_computation.2 | async-start | bytes 524288 | tf_op jit(solution)/shard_map/all_to_all | solution.py:14
  65.1 12.6 %all-to-all-done.2 = f32[64,8,128]{2,1,0:T(8,128)S(1)} async-done(((f32[64,8,128]{2,1,0:T(8,128)}), f32[64,8,128]{2,1,0:T(8,128)S(1)}, u32[]{:S(2)}, u32[]{:S(2)}) %all-to-all-start.2) | async-done | bytes 262176 | tf_op jit(solution)/shard_map/all_to_all | solution.py:14
  77.7 0.2 copy.10
  78.0 0.1 copy.11
  78.1 5.8 %cholesky.15 = f32[64,64]{1,0:T(8,128)S(1)} custom-call(f32[64,64]{1,0:T(8,128)S(1)} %fusion.17), custom_call_target="Cholesky" | custom-call | tf_op jit(solution)/shard_map/jit(cholesky)/cholesky | solution.py:42
  84.0 0.6 compare_reduce_fusion
  84.6 0.7 fusion.14
  85.3 4.9 %custom-call.7 = f32[1,64,64]{1,2,0:T(8,128)S(1)} custom-call(f32[1,64,64]{2,1,0:T(8,128)S(1)} %fusion.14), custom_call_target="InvertDiagBlocksLowerTriangular" | custom-call | tf_op jit(solution)/shard_map/jit(_solve_triangular)/triangular_solve | solution.py:44
  90.2 0.7 fusion.2
  90.9 0.1 multiply_reduce_fusion
  91.0 0.6 broadcast_in_dim_broadcast_in_dim_broadcast_in_dim.2
  91.7 6.7 %all-to-all-start.3 = ((f32[16,8,128]{2,1,0:T(8,128)}), f32[16,8,128]{2,1,0:T(8,128)S(1)}, u32[]{:S(2)}, u32[]{:S(2)}) async-start(f32[16,8,128]{2,1,0:T(8,128)} %broadcast_in_dim_broadcast_in_dim_broadcast_in_dim.2), calls=%async_computation.3 | async-start | bytes 131072 | tf_op jit(solution)/shard_map/all_to_all | solution.py:14
  98.3 1.1 %fusion = f32[64,896]{1,0:T(8,128)} fusion(f32[64,896]{1,0:T(8,128)S(1)} %convert_add_fusion, f32[64,960]{1,0:T(8,128)S(1)} %fusion.2), kind=kOutput, calls=%fused_computation.2 | convolution fusion | flops 44154880 | bytes 704512 | tf_op jit(solution)/shard_map/dot_general | solution.py:52
  99.4 6.8 %all-to-all-done.3 = f32[16,8,128]{2,1,0:T(8,128)S(1)} async-done(((f32[16,8,128]{2,1,0:T(8,128)}), f32[16,8,128]{2,1,0:T(8,128)S(1)}, u32[]{:S(2)}, u32[]{:S(2)}) %all-to-all-start.3) | async-done | bytes 65568 | tf_op jit(solution)/shard_map/all_to_all | solution.py:14
  106.2 0.0 copy-start.1
  106.2 0.8 fusion.20
  107.0 0.2 copy-done.1
  107.1 1.1 %fusion.1 = f32[64,896]{1,0:T(8,128)} fusion(f32[64,896]{1,0:T(8,128)S(1)} %copy-done.1, f32[64,960]{1,0:T(8,128)S(1)} %fusion.2, f32[64]{0:T(128)S(1)} %add_bitcast_fusion), kind=kOutput, calls=%fused_computation.4 | convolution fusion | flops 44212224 | bytes 704768 | tf_op jit(solution)/shard_map/dot_general | solution.py:56
  (13 shorter events, 0.2 us)
Async XLA Ops:
  0.6 1.1 %copy-start = (f32[896,64]{0,1:T(8,128)S(1)}, f32[896,64]{0,1:T(8,128)}, u32[]{:S(2)}) copy-start(f32[896,64]{0,1:T(8,128)} %param.7) | copy-start | bytes 688132
  60.3 17.4 %all-to-all-start.2 = ((f32[64,8,128]{2,1,0:T(8,128)}), f32[64,8,128]{2,1,0:T(8,128)S(1)}, u32[]{:S(2)}, u32[]{:S(2)}) async-start(f32[64,8,128]{2,1,0:T(8,128)} %broadcast_in_dim.9), calls=%async_computation.2 | async-start | bytes 524288 | tf_op jit(solution)/shard_map/all_to_all | solution.py:14
  91.7 14.5 %all-to-all-start.3 = ((f32[16,8,128]{2,1,0:T(8,128)}), f32[16,8,128]{2,1,0:T(8,128)S(1)}, u32[]{:S(2)}, u32[]{:S(2)}) async-start(f32[16,8,128]{2,1,0:T(8,128)} %broadcast_in_dim_broadcast_in_dim_broadcast_in_dim.2), calls=%async_computation.3 | async-start | bytes 131072 | tf_op jit(solution)/shard_map/all_to_all | solution.py:14
  106.2 0.9 copy-start.1

commit v2 on v1

v2 whole, which is shorter than its diff:
```python
import math

import jax
import jax.numpy as jnp
from jax import lax
from jax.experimental import pallas as pl
from jax.experimental.pallas import tpu as pltpu
from jax.sharding import PartitionSpec as P

decay_rate = 0.95
step_size = 0.3
tiny_eps = 1e-08
highest = lax.Precision.HIGHEST
f32 = jnp.float32


def exchange(blocks, axis):
    return lax.all_to_all(blocks, axis, 0, 0)


def copies(block, axis):
    return jnp.broadcast_to(block[None], (lax.axis_size(axis),) + block.shape)


def eliminate(blocks, size, width):
    sublane = lax.broadcasted_iota(jnp.int32, (8, width), 0)

    def spread_row(block, row):
        return jnp.broadcast_to(block[row:row + 1, :], (8, width))

    def spread_column(block, column):
        return jnp.broadcast_to(block[:, column:column + 1], (8, width))

    count = size // 8
    for first in range(count):
        live = range(first, count)
        columns = [{i: spread_column(blocks[i], 8 * first + k) for i in live} for k in range(8)]
        for k in range(8):
            inverse = 1.0 / spread_row(columns[k][first], k)
            row = spread_row(blocks[first], k)
            ratio = {i: columns[k][i] * inverse for i in live}
            ratio[first] = jnp.where(sublane > k, ratio[first], 0.0)
            for later in range(k + 1, 8):
                entry = spread_row(columns[later][first], k)
                for i in live:
                    columns[later][i] = columns[later][i] - ratio[i] * entry
            for i in live:
                if i > first or k < 7:
                    blocks[i] = blocks[i] - ratio[i] * row
    return blocks


def factor_kernel(whole_ref, left_ref, right_ref, ortho_ref, squares_ref):
    rank = left_ref.shape[1]
    slabs = right_ref.shape[1] // 128
    row = lax.broadcasted_iota(jnp.int32, (rank, 2 * rank), 0)
    column = lax.broadcasted_iota(jnp.int32, (rank, 2 * rank), 1)
    start = jnp.where(column < rank, whole_ref[:, slabs, :], jnp.where(column == row + rank, 1.0, 0.0))
    blocks = eliminate([start[8 * i:8 * i + 8] for i in range(rank // 8)], rank, 2 * rank)
    done = jnp.concatenate(blocks, axis=0)
    pivots = jnp.sum(jnp.where(row == column, done, 0.0), axis=1, keepdims=True)
    inverse = (done / jnp.sqrt(pivots))[:, rank:]
    total = jnp.zeros((rank, 128), f32)
    for slab in range(slabs):
        right = jnp.dot(inverse, whole_ref[:, slab, :], precision=highest, preferred_element_type=f32)
        right_ref[:, 128 * slab:128 * slab + 128] = right
        total = total + right * right
    by_columns = (((1,), (1,)), ((), ()))
    ortho_ref[...] = lax.dot_general(left_ref[...], inverse, by_columns, precision=highest, preferred_element_type=f32)
    squares = lax.dot_general(jnp.ones((8, 128), f32), total, by_columns, precision=highest, preferred_element_type=f32)
    squares_ref[...] = jnp.concatenate([squares, jnp.zeros((8, 128 - rank), f32)], axis=1)


def per_device(weight, momentum, gradient, right_basis):
    rank = right_basis.shape[1]
    rows, cols = weight.shape
    buffer = momentum + gradient.astype(f32)
    left_part = jnp.dot(buffer, right_basis, precision=highest)
    half = rows // 2
    packed = jnp.concatenate([left_part[:half], left_part[half:]], axis=1)
    packed = jnp.sum(exchange(copies(packed, "tensor"), "tensor"), axis=0)
    left = jnp.concatenate([packed[:, :rank], packed[:, rank:]], axis=0)
    wide = jnp.concatenate([buffer, left, jnp.zeros((rows, 1024 - cols - rank), f32)], axis=1)
    products = jnp.dot(left.T, wide, precision=highest).reshape(rank, 8, 128)
    mine = jnp.sum(exchange(products, "fsdp"), axis=0)
    whole = exchange(copies(mine, "fsdp"), "fsdp")
    in_vmem = pl.BlockSpec(memory_space=pltpu.VMEM)
    right_t, ortho, squares = pl.pallas_call(
        factor_kernel,
        out_shape=[
            jax.ShapeDtypeStruct((rank, cols), f32),
            jax.ShapeDtypeStruct((rows, rank), f32),
            jax.ShapeDtypeStruct((8, 128), f32),
        ],
        in_specs=[in_vmem] * 2,
        out_specs=[in_vmem] * 3,
        name="factor",
    )(whole, left)
    squares = jnp.sum(exchange(copies(squares, "tensor"), "tensor"), axis=0)
    norms = jnp.sqrt(squares[0, :rank])
    new_basis = right_t.T / (norms + tiny_eps)
    new_momentum = buffer - (1.0 - decay_rate) * jnp.dot(ortho, right_t, precision=highest)
    total_rows = rows * lax.axis_size("fsdp")
    total_cols = cols * lax.axis_size("tensor")
    factor = step_size * math.sqrt(total_rows * total_cols / rank)
    new_weight = weight - factor * jnp.dot(ortho, new_basis.T, precision=highest)
    return (new_weight, new_momentum, new_basis)


def solution(mesh):
    placed = (P("fsdp", "tensor"), P("fsdp", "tensor"), P("fsdp", "tensor"), P("tensor", None))
    return jax.shard_map(
        per_device,
        mesh=mesh,
        in_specs=placed,
        out_specs=(P("fsdp", "tensor"), P("fsdp", "tensor"), P("tensor", None)),
        check_vma=False,
    )
```

time: 109 us -> 102 us (0.936)
  blocking collectives: 56.7 us -> 27 us
  starting transfers between devices: 11.5 us -> 29.8 us
  other arithmetic: 14.2 us -> 2.66 us
  waiting for transfers between devices: 19.3 us -> 29.4 us
  Pallas kernels: 0 us -> 3.97 us
  local copies, waits for them, and re-layouts: 2.02 us -> 3.85 us
    all_to_all x2 -> x1, blocking collectives: 56.7 us -> 27 us  [exchange(): return lax.all_to_all(blocks, axis, 0, 0)]
    all_to_all x2 -> x3, starting transfers between devices: 11.5 us -> 29.8 us  [exchange(): return lax.all_to_all(blocks, axis, 0, 0)]
    another operation x5 -> x0, other arithmetic: 12.1 us -> none  [the longest x3 6.52 us: per_device(): lower_factor = jnp.linalg.cholesky(gram_matrix)]
    all_to_all x2 -> x3, waiting for transfers between devices: 19.3 us -> 29.4 us  [exchange(): return lax.all_to_all(blocks, axis, 0, 0)]
    pallas_call x0 -> x1, Pallas kernels: none -> 3.97 us  [per_device(): pl.pallas_call(factor_kernel, out_shape=[jax.ShapeDtypeStruct((rank, cols...]
    broadcast_in_dim x3 -> x4, local copies, waits for them, and re-layouts: 0.74 us -> 2.76 us  [the longest x3 2.76 us: copies(): return jnp.broadcast_to(block[None], (lax.axis_size(axis),) + block.shape)]
  transfers between devices with their start and end apart: 2 -> 3, of which waited for: 2 -> 3; matrix products, arithmetic and copies ran while one was open for 1% -> 3% of each run, Pallas kernels for 0% -> 0%
where the time goes in v2:
time: 102 us; the launch traced here: 101 us
  starting transfers between devices  29.8 us (29%)
  waiting for transfers between devices  29.4 us (29%)
  blocking collectives  27 us (26%)
  Pallas kernels  3.97 us (4%)
  matrix products  3.91 us (4%)
  local copies, waits for them, and re-layouts  3.85 us (4%)
  other arithmetic  2.66 us (3%)
    all_to_all x3, starting transfers between devices, exchange(): return lax.all_to_all(blocks, axis, 0, 0)  29.8 us
    all_to_all x3, waiting for transfers between devices, exchange(): return lax.all_to_all(blocks, axis, 0, 0)  29.4 us
    all_to_all x1, blocking collectives, exchange(): return lax.all_to_all(blocks, axis, 0, 0)  27 us
    pallas_call x1, Pallas kernels, per_device(): pl.pallas_call(factor_kernel, out_shape=[jax.ShapeDtypeStruct((rank, cols...  3.97 us
    broadcast_in_dim x3, local copies, waits for them, and re-layouts, copies(): return jnp.broadcast_to(block[None], (lax.axis_size(axis),) + block.shape)  2.76 us
  transfers between devices with their start and end apart: 3, of which 3 were waited for; matrix products, arithmetic and copies ran while one was open for 3% of the time, Pallas kernels for 0%

profile of v2, /device:TPU:1, one launch (start us, length us, event | category | flops | bytes accessed | tf_op | source)
XLA Modules:
  0.0 101.3 jit_solution(15094887773500570371)
XLA Ops:
  0.6 0.0 copy-start
  0.6 1.1 %convert_add_fusion = f32[64,896]{1,0:T(8,128)S(1)} fusion(f32[64,896]{1,0:T(8,128)} %param.5, bf16[64,896]{1,0:T(8,128)(2,1)} %param.6), kind=kLoop, calls=%fused_computation.11 | loop fusion | flops 114688 | bytes 573440 | tf_op jit(solution)/shard_map/add | solution.py:77
  1.7 0.0 copy-done
  1.7 0.4 fusion.13
  2.1 0.1 pad_maximum_fusion.1
  2.2 0.7 broadcast_in_dim.8
  2.9 18.2 %all-to-all-start = ((f32[16,32,128]{2,1,0:T(8,128)}), f32[16,32,128]{2,1,0:T(8,128)S(1)}, u32[]{:S(2)}, u32[]{:S(2)}) async-start(f32[16,32,128]{2,1,0:T(8,128)} %broadcast_in_dim.8), calls=%async_computation | async-start | bytes 524288 | tf_op jit(solution)/shard_map/all_to_all | solution.py:18
  21.1 0.1 pad.3.clone
  21.2 11.6 %all-to-all-done = f32[16,32,128]{2,1,0:T(8,128)S(1)} async-done(((f32[16,32,128]{2,1,0:T(8,128)}), f32[16,32,128]{2,1,0:T(8,128)S(1)}, u32[]{:S(2)}, u32[]{:S(2)}) %all-to-all-start) | async-done | bytes 262176 | tf_op jit(solution)/shard_map/all_to_all | solution.py:18
  32.9 0.1 fusion.12
  32.9 0.4 convolution_bitcast_fusion
  33.4 27.0 %all_to_all.20 = f32[64,8,128]{2,1,0:T(8,128)S(1)} all-to-all(f32[64,8,128]{2,1,0:T(8,128)S(1)} %bitcast.12), channel_id=1, replica_groups=mesh['fsdp'=64,'tensor'=16] {'fsdp'}, dimensions={0} | all-to-all | bytes 524288 | tf_op jit(solution)/shard_map/all_to_all | solution.py:18
  60.4 0.1 reduce_sum.28
  60.5 0.7 broadcast_in_dim.10
  61.2 4.9 %all-to-all-start.2 = ((f32[64,8,128]{2,1,0:T(8,128)}), f32[64,8,128]{2,1,0:T(8,128)S(1)}, u32[]{:S(2)}, u32[]{:S(2)}) async-start(f32[64,8,128]{2,1,0:T(8,128)} %broadcast_in_dim.10), calls=%async_computation.2 | async-start | bytes 524288 | tf_op jit(solution)/shard_map/all_to_all | solution.py:18
  66.0 0.6 pad_maximum_fusion.left_ref
  66.7 12.0 %all-to-all-done.2.whole_ref = f32[64,8,128]{2,1,0:T(8,128)S(1)} async-done(((f32[64,8,128]{2,1,0:T(8,128)}), f32[64,8,128]{2,1,0:T(8,128)S(1)}, u32[]{:S(2)}, u32[]{:S(2)}) %all-to-all-start.2) | async-done | bytes 262176 | tf_op jit(solution)/shard_map/all_to_all | solution.py:18
  78.6 0.0 copy-start.1
  78.6 0.7 copy-done.1
  79.3 4.0 %factor.1 = (f32[64,896]{1,0:T(8,128)}, f32[64,64]{1,0:T(8,128)}, f32[8,128]{1,0:T(8,128)}) custom-call(f32[64,8,128]{2,1,0:T(8,128)} %copy-done.1, f32[64,64]{1,0:T(8,128)} %pad_maximum_fusion.left_ref), custom_call_target="tpu_custom_call" | custom-call | tf_op jit(solution)/shard_map/factor/pallas_call | solution.py:88
  83.3 1.3 %broadcast_in_dim.11 = f32[16,8,128]{2,1,0:T(8,128)} broadcast(f32[8,128]{1,0:T(8,128)} %get-tuple-element.8), dimensions={1,2} | broadcast | bytes 69632 | tf_op jit(solution)/shard_map/broadcast_in_dim | solution.py:22
  84.6 0.0 copy-start.3
  84.6 6.8 %all-to-all-start.3 = ((f32[16,8,128]{2,1,0:T(8,128)}), f32[16,8,128]{2,1,0:T(8,128)S(1)}, u32[]{:S(2)}, u32[]{:S(2)}) async-start(f32[16,8,128]{2,1,0:T(8,128)} %broadcast_in_dim.11), calls=%async_computation.3 | async-start | bytes 131072 | tf_op jit(solution)/shard_map/all_to_all | solution.py:18
  91.4 0.0 copy-done.3
  91.4 0.0 copy-start.2
  91.4 2.0 %fusion = f32[64,896]{1,0:T(8,128)} fusion(f32[64,896]{1,0:T(8,128)S(1)} %convert_add_fusion, f32[64,64]{1,0:T(8,128)S(1)} %copy-done.3, f32[64,896]{1,0:T(8,128)} %get-tuple-element.7), kind=kOutput, calls=%fused_computation.2 | convolution fusion | flops 44154880 | bytes 704512 | tf_op jit(solution)/shard_map/dot_general | solution.py:102
  93.4 5.8 %all-to-all-done.3 = f32[16,8,128]{2,1,0:T(8,128)S(1)} async-done(((f32[16,8,128]{2,1,0:T(8,128)}), f32[16,8,128]{2,1,0:T(8,128)S(1)}, u32[]{:S(2)}, u32[]{:S(2)}) %all-to-all-start.3) | async-done | bytes 65568 | tf_op jit(solution)/shard_map/all_to_all | solution.py:18
  99.3 0.0 copy-done.2
  99.3 0.0 copy-start.4
  99.3 0.8 fusion.9
  100.1 0.2 copy-done.4
  100.2 1.1 %fusion.1 = f32[64,896]{1,0:T(8,128)} fusion(f32[64,896]{1,0:T(8,128)S(1)} %copy-done.4, f32[64,64]{1,0:T(8,128)S(1)} %copy-done.3, f32[64,896]{1,0:T(8,128)S(1)} %copy-done.2, f32[64]{0:T(128)S(1)} %add_bitcast_fusion), kind=kOutput, calls=%fused_computation.4 | convolution fusion | flops 44212224 | bytes 704768 | tf_op jit(solution)/shard_map/dot_general | solution.py:106
  (6 shorter events, 0.1 us)
Async XLA Ops:
  0.6 1.1 %copy-start = (f32[896,64]{0,1:T(8,128)S(1)}, f32[896,64]{0,1:T(8,128)}, u32[]{:S(2)}) copy-start(f32[896,64]{0,1:T(8,128)} %param.7) | copy-start | bytes 688132
  2.9 29.9 %all-to-all-start = ((f32[16,32,128]{2,1,0:T(8,128)}), f32[16,32,128]{2,1,0:T(8,128)S(1)}, u32[]{:S(2)}, u32[]{:S(2)}) async-start(f32[16,32,128]{2,1,0:T(8,128)} %broadcast_in_dim.8), calls=%async_computation | async-start | bytes 524288 | tf_op jit(solution)/shard_map/all_to_all | solution.py:18
  61.2 17.4 %all-to-all-start.2 = ((f32[64,8,128]{2,1,0:T(8,128)}), f32[64,8,128]{2,1,0:T(8,128)S(1)}, u32[]{:S(2)}, u32[]{:S(2)}) async-start(f32[64,8,128]{2,1,0:T(8,128)} %broadcast_in_dim.10), calls=%async_computation.2 | async-start | bytes 524288 | tf_op jit(solution)/shard_map/all_to_all | solution.py:18
  78.6 0.7 copy-start.1
  84.6 6.8 %copy-start.3 = (f32[64,64]{1,0:T(8,128)S(1)}, f32[64,64]{1,0:T(8,128)}, u32[]{:S(2)}) copy-start(f32[64,64]{1,0:T(8,128)} %get-tuple-element.6) | copy-start | bytes 49156
  84.6 14.6 %all-to-all-start.3 = ((f32[16,8,128]{2,1,0:T(8,128)}), f32[16,8,128]{2,1,0:T(8,128)S(1)}, u32[]{:S(2)}, u32[]{:S(2)}) async-start(f32[16,8,128]{2,1,0:T(8,128)} %broadcast_in_dim.11), calls=%async_computation.3 | async-start | bytes 131072 | tf_op jit(solution)/shard_map/all_to_all | solution.py:18
  91.4 7.9 %copy-start.2 = (f32[64,896]{1,0:T(8,128)S(1)}, f32[64,896]{1,0:T(8,128)}, u32[]{:S(2)}) copy-start(f32[64,896]{1,0:T(8,128)} %get-tuple-element.7) | copy-start | bytes 688132
  99.3 0.9 copy-start.4

commit v3 on v2

v3 whole, which is shorter than its diff:
```python
import functools
import math

import jax
import jax.numpy as jnp
from jax import lax
from jax.experimental import pallas as pl
from jax.experimental.pallas import tpu as pltpu
from jax.sharding import PartitionSpec as P

decay_rate = 0.95
step_size = 0.3
tiny_eps = 1e-08
highest = lax.Precision.HIGHEST
f32 = jnp.float32


def exchange(blocks, axis):
    return lax.all_to_all(blocks, axis, 0, 0)


def copies(block, axis):
    return jnp.broadcast_to(block[None], (lax.axis_size(axis),) + block.shape)


def eliminate(blocks, size, width):
    sublane = lax.broadcasted_iota(jnp.int32, (8, width), 0)

    def spread_row(block, row):
        return jnp.broadcast_to(block[row:row + 1, :], (8, width))

    def spread_column(block, column):
        return jnp.broadcast_to(block[:, column:column + 1], (8, width))

    count = size // 8
    for first in range(count):
        live = range(first, count)
        columns = [{i: spread_column(blocks[i], 8 * first + k) for i in live} for k in range(8)]
        for k in range(8):
            inverse = 1.0 / spread_row(columns[k][first], k)
            row = spread_row(blocks[first], k)
            ratio = {i: columns[k][i] * inverse for i in live}
            ratio[first] = jnp.where(sublane > k, ratio[first], 0.0)
            for later in range(k + 1, 8):
                entry = spread_row(columns[later][first], k)
                for i in live:
                    columns[later][i] = columns[later][i] - ratio[i] * entry
            for i in live:
                if i > first or k < 7:
                    blocks[i] = blocks[i] - ratio[i] * row
    return blocks


def dot(a, b, contract=((1,), (0,)), precision=highest):
    return lax.dot_general(a, b, (contract, ((), ())), precision=precision, preferred_element_type=f32)


def left_kernel(momentum_ref, gradient_ref, basis_ref, buffer_ref, copies_ref):
    buffer = momentum_ref[...] + gradient_ref[...].astype(f32)
    buffer_ref[...] = buffer
    part = dot(buffer, basis_ref[...], ((1,), (1,)))
    half = part.shape[0] // 2
    packed = jnp.concatenate([part[:half], part[half:]], axis=1)
    copies_ref[...] = jnp.broadcast_to(packed[None], copies_ref.shape)


def product_kernel(parts_ref, buffer_ref, left_ref, products_ref):
    rank = left_ref.shape[1]
    packed = jnp.sum(parts_ref[...], axis=0)
    left = jnp.concatenate([packed[:, :rank], packed[:, rank:]], axis=0)
    left_ref[...] = left
    turned = left.T
    slabs = buffer_ref.shape[1] // 128
    for slab in range(slabs):
        products_ref[:, slab, :] = dot(turned, buffer_ref[:, 128 * slab:128 * slab + 128])
    gram = dot(turned, left)
    products_ref[:, slabs, :] = jnp.concatenate([gram, jnp.zeros((rank, 128 - rank), f32)], axis=1)


def factor_kernel(whole_ref, left_ref, right_ref, ortho_ref, copies_ref):
    rank = left_ref.shape[1]
    slabs = right_ref.shape[1] // 128
    row = lax.broadcasted_iota(jnp.int32, (rank, 2 * rank), 0)
    column = lax.broadcasted_iota(jnp.int32, (rank, 2 * rank), 1)
    start = jnp.where(column < rank, whole_ref[:, slabs, :], jnp.where(column == row + rank, 1.0, 0.0))
    blocks = eliminate([start[8 * i:8 * i + 8] for i in range(rank // 8)], rank, 2 * rank)
    done = jnp.concatenate(blocks, axis=0)
    pivots = jnp.sum(jnp.where(row == column, done, 0.0), axis=1, keepdims=True)
    inverse = (done / jnp.sqrt(pivots))[:, rank:]
    total = jnp.zeros((rank, 128), f32)
    for slab in range(slabs):
        right = dot(inverse, whole_ref[:, slab, :])
        right_ref[:, 128 * slab:128 * slab + 128] = right
        total = total + right * right
    squares = dot(jnp.ones((8, 128), f32), total, ((1,), (1,)))
    squares = jnp.concatenate([squares, jnp.zeros((8, 128 - rank), f32)], axis=1)
    copies_ref[...] = jnp.broadcast_to(squares[None], copies_ref.shape)
    ortho_ref[...] = dot(left_ref[...], inverse, ((1,), (1,)))


def update_kernel(factor, squares_ref, right_ref, ortho_ref, buffer_ref, weight_ref,
                  new_weight_ref, new_momentum_ref, new_basis_ref):
    rows, rank = ortho_ref.shape
    norms = jnp.sqrt(jnp.sum(squares_ref[...], axis=0))[:1, :rank]
    scale = 1.0 / (norms + tiny_eps)
    row = lax.broadcasted_iota(jnp.int32, (rank, rank), 0)
    column = lax.broadcasted_iota(jnp.int32, (rank, rank), 1)
    turned = jnp.sum(jnp.where(row == column, scale, 0.0), axis=1, keepdims=True)
    right = right_ref[...]
    ortho = ortho_ref[...]
    both = jnp.concatenate([(1.0 - decay_rate) * ortho, factor * (ortho * scale)], axis=0)
    both_high = both.astype(jnp.bfloat16)
    both_low = (both - both_high.astype(f32)).astype(jnp.bfloat16)
    right_high = right.astype(jnp.bfloat16)
    right_low = (right - right_high.astype(f32)).astype(jnp.bfloat16)
    update = dot(
        jnp.concatenate([both_high, both_low, both_high], axis=1),
        jnp.concatenate([right_high, right_high, right_low], axis=0),
        precision=lax.Precision.DEFAULT,
    )
    new_momentum_ref[...] = buffer_ref[...] - update[:rows]
    new_weight_ref[...] = weight_ref[...] - update[rows:]
    new_basis_ref[...] = right * turned


def call(kernel, name, args, shapes):
    in_vmem = pl.BlockSpec(memory_space=pltpu.VMEM)
    return pl.pallas_call(
        kernel,
        out_shape=[jax.ShapeDtypeStruct(shape, f32) for shape in shapes],
        in_specs=[in_vmem] * len(args),
        out_specs=[in_vmem] * len(shapes),
        name=name,
    )(*args)


def per_device(weight, momentum, gradient, right_basis):
    rank = right_basis.shape[1]
    rows, cols = weight.shape
    fsdp, tensor = lax.axis_size("fsdp"), lax.axis_size("tensor")
    buffer, parts = call(
        left_kernel, "left", (momentum, gradient, right_basis.T),
        [(rows, cols), (tensor, rows // 2, 2 * rank)])
    parts = exchange(parts, "tensor")
    left, products = call(product_kernel, "products", (parts, buffer), [(rows, rank), (rank, 8, 128)])
    mine = jnp.sum(exchange(products, "fsdp"), axis=0)
    whole = exchange(copies(mine, "fsdp"), "fsdp")
    right, ortho, squares = call(
        factor_kernel, "factor", (whole, left),
        [(rank, cols), (rows, rank), (tensor, 8, 128)])
    squares = exchange(squares, "tensor")
    factor = step_size * math.sqrt(rows * fsdp * cols * tensor / rank)
    new_weight, new_momentum, new_basis = call(
        functools.partial(update_kernel, factor), "update", (squares, right, ortho, buffer, weight),
        [(rows, cols), (rows, cols), (rank, cols)])
    return (new_weight, new_momentum, new_basis.T)


def solution(mesh):
    placed = (P("fsdp", "tensor"), P("fsdp", "tensor"), P("fsdp", "tensor"), P("tensor", None))
    return jax.shard_map(
        per_device,
        mesh=mesh,
        in_specs=placed,
        out_specs=(P("fsdp", "tensor"), P("fsdp", "tensor"), P("tensor", None)),
        check_vma=False,
    )
```

time: 102 us -> 102 us (level)
  blocking collectives: 27 us -> 89.7 us
  starting transfers between devices: 29.8 us -> 0 us
  waiting for transfers between devices: 29.4 us -> 0 us
  Pallas kernels: 3.97 us -> 10.9 us
  matrix products: 3.91 us -> 0 us
  local copies, waits for them, and re-layouts: 3.85 us -> 0.02 us
  other arithmetic: 2.66 us -> 0.07 us
    all_to_all x1 -> x4, blocking collectives: 27 us -> 89.7 us  [exchange(): return lax.all_to_all(blocks, axis, 0, 0)]
    all_to_all x3 -> x0, starting transfers between devices: 29.8 us -> none  [exchange(): return lax.all_to_all(blocks, axis, 0, 0)]
    all_to_all x3 -> x0, waiting for transfers between devices: 29.4 us -> none  [exchange(): return lax.all_to_all(blocks, axis, 0, 0)]
    pallas_call x1 -> x4, Pallas kernels: 3.97 us -> 10.9 us  [call(): pl.pallas_call(kernel, out_shape=[jax.ShapeDtypeStruct(shape, f32) for sh...]
    dot_general x4 -> x0, matrix products: 3.91 us -> none  [the longest x1 2.02 us: per_device(): jnp.dot(ortho, right_t, precision=highest)]
    broadcast_in_dim x3 -> x1, local copies, waits for them, and re-layouts: 2.76 us -> 0.02 us  [copies(): return jnp.broadcast_to(block[None], (lax.axis_size(axis),) + block.shape)]
    add x1 -> x0, other arithmetic: 1.07 us -> none  [per_device(): buffer = momentum + gradient.astype(f32)]
  transfers between devices with their start and end apart: 3 -> 0, of which waited for: 3 -> 0; matrix products, arithmetic and copies ran while one was open for 3% -> 0% of each run, Pallas kernels for 0% -> 0%
where the time goes in v3:
time: 102 us; the launch traced here: 101 us
  blocking collectives  89.7 us (88%)
  Pallas kernels  10.9 us (11%)
    all_to_all x4, blocking collectives, exchange(): return lax.all_to_all(blocks, axis, 0, 0)  89.7 us
    pallas_call x4, Pallas kernels, call(): pl.pallas_call(kernel, out_shape=[jax.ShapeDtypeStruct(shape, f32) for sh...  10.9 us

profile of v3, /device:TPU:1, one launch (start us, length us, event | category | flops | bytes accessed | tf_op | source)
XLA Modules:
  0.0 101.3 jit_solution(1929871027291305613)
XLA Ops:
  0.6 2.3 %left.1 = (f32[64,896]{1,0:T(8,128)}, f32[16,32,128]{2,1,0:T(8,128)}) custom-call(f32[64,896]{1,0:T(8,128)} %momentum_ref.1, bf16[64,896]{1,0:T(8,128)(2,1)} %gradient_ref.1, f32[64,896]{1,0:T(8,128)} %bitcast.2), custom_call_target="tpu_custom_call" | custom-call | tf_op jit(solution)/shard_map/left/pallas_call | solution.py:128
  2.9 30.0 %all_to_all.20.parts_ref = f32[16,32,128]{2,1,0:T(8,128)} all-to-all(f32[16,32,128]{2,1,0:T(8,128)} %get-tuple-element.13), channel_id=1, replica_groups=mesh['fsdp'=64,'tensor'=16] {'tensor'}, dimensions={0} | all-to-all | bytes 524288 | tf_op jit(solution)/shard_map/all_to_all | solution.py:19
  32.9 2.2 %products.1 = (f32[64,64]{1,0:T(8,128)}, f32[64,8,128]{2,1,0:T(8,128)}) custom-call(f32[16,32,128]{2,1,0:T(8,128)} %all_to_all.20.parts_ref, f32[64,896]{1,0:T(8,128)} %get-tuple-element.14.buffer_ref), custom_call_target="tpu_custom_call" | custom-call | tf_op jit(solution)/shard_map/products/pallas_call | solution.py:128
  35.1 27.2 %all_to_all.21 = f32[64,8,128]{2,1,0:T(8,128)S(1)} all-to-all(f32[64,8,128]{2,1,0:T(8,128)} %get-tuple-element.15), channel_id=1, replica_groups=mesh['fsdp'=64,'tensor'=16] {'fsdp'}, dimensions={0} | all-to-all | bytes 524288 | tf_op jit(solution)/shard_map/all_to_all | solution.py:19
  62.3 0.1 reduce_sum.9
  62.4 17.3 %all_to_all.22.whole_ref = f32[64,8,128]{2,1,0:T(8,128)} all-to-all(f32[64,8,128]{2,1,0:T(8,128)S(1)} %broadcast_in_dim.2), channel_id=1, replica_groups=mesh['fsdp'=64,'tensor'=16] {'fsdp'}, dimensions={0} | all-to-all | bytes 524288 | tf_op jit(solution)/shard_map/all_to_all | solution.py:19
  79.8 4.1 %factor.1 = (f32[64,896]{1,0:T(8,128)}, f32[64,64]{1,0:T(8,128)}, f32[16,8,128]{2,1,0:T(8,128)}) custom-call(f32[64,8,128]{2,1,0:T(8,128)} %all_to_all.22.whole_ref, f32[64,64]{1,0:T(8,128)} %get-tuple-element.16.left_ref), custom_call_target="tpu_custom_call" | custom-call | tf_op jit(solution)/shard_map/factor/pallas_call | solution.py:128
  83.8 15.1 %all_to_all.23.squares_ref = f32[16,8,128]{2,1,0:T(8,128)} all-to-all(f32[16,8,128]{2,1,0:T(8,128)} %get-tuple-element.17), channel_id=1, replica_groups=mesh['fsdp'=64,'tensor'=16] {'tensor'}, dimensions={0} | all-to-all | bytes 131072 | tf_op jit(solution)/shard_map/all_to_all | solution.py:19
  99.0 2.3 %update.1 = (f32[64,896]{1,0:T(8,128)}, f32[64,896]{1,0:T(8,128)}, f32[64,896]{1,0:T(8,128)}) custom-call(f32[16,8,128]{2,1,0:T(8,128)} %all_to_all.23.squares_ref, f32[64,896]{1,0:T(8,128)} %get-tuple-element.18.right_ref, f32[64,64]{1,0:T(8,128)} %get-tuple-element.19.ortho_ref, f32[64,896]{1,0:T(8,128)} %get-tuple-element.14.buffer_ref, f32[64,896]{1,0:T(8,128)} %weight_ref.1), custom_call_target="tpu_custom_call" | custom-call | tf_op jit(solution)/shard_map/update/pallas_call | solution.py:128
  (1 shorter events, 0.0 us)

commit v4 on v3

--- a/solution.py
+++ b/solution.py
@@ -55,10 +55,26 @@
     return lax.dot_general(a, b, (contract, ((), ())), precision=precision, preferred_element_type=f32)
 
 
-def left_kernel(momentum_ref, gradient_ref, basis_ref, buffer_ref, copies_ref):
-    buffer = momentum_ref[...] + gradient_ref[...].astype(f32)
-    buffer_ref[...] = buffer
-    part = dot(buffer, basis_ref[...], ((1,), (1,)))
+def terms(x, count):
+    parts = []
+    for _ in range(count):
+        parts.append(x.astype(jnp.bfloat16))
+        x = x - parts[-1].astype(f32)
+    return parts
+
+
+def stacked(a, b, depth):
+    a, b = terms(a, depth), terms(b, depth)
+    pairs = [(i, j) for i in range(depth) for j in range(depth) if i + j < depth]
+    return dot(
+        jnp.concatenate([a[i] for i, _ in pairs], axis=1),
+        jnp.concatenate([b[j] for _, j in pairs], axis=0),
+        precision=lax.Precision.DEFAULT,
+    )
+
+
+def left_kernel(buffer_ref, basis_ref, copies_ref):
+    part = dot(buffer_ref[...], basis_ref[...], ((1,), (1,)))
     half = part.shape[0] // 2
     packed = jnp.concatenate([part[:half], part[half:]], axis=1)
     copies_ref[...] = jnp.broadcast_to(packed[None], copies_ref.shape)
@@ -69,12 +85,10 @@
     packed = jnp.sum(parts_ref[...], axis=0)
     left = jnp.concatenate([packed[:, :rank], packed[:, rank:]], axis=0)
     left_ref[...] = left
-    turned = left.T
-    slabs = buffer_ref.shape[1] // 128
-    for slab in range(slabs):
-        products_ref[:, slab, :] = dot(turned, buffer_ref[:, 128 * slab:128 * slab + 128])
-    gram = dot(turned, left)
-    products_ref[:, slabs, :] = jnp.concatenate([gram, jnp.zeros((rank, 128 - rank), f32)], axis=1)
+    padded = jnp.concatenate([left, jnp.zeros((left.shape[0], 128 - rank), f32)], axis=1)
+    products = stacked(left.T, jnp.concatenate([buffer_ref[...], padded], axis=1), 3)
+    slabs = [products[:, i:i + 128] for i in range(0, products.shape[1], 128)]
+    products_ref[...] = jnp.swapaxes(jnp.stack(slabs, axis=0), 0, 1)
 
 
 def factor_kernel(whole_ref, left_ref, right_ref, ortho_ref, copies_ref):
@@ -87,11 +101,9 @@
     done = jnp.concatenate(blocks, axis=0)
     pivots = jnp.sum(jnp.where(row == column, done, 0.0), axis=1, keepdims=True)
     inverse = (done / jnp.sqrt(pivots))[:, rank:]
-    total = jnp.zeros((rank, 128), f32)
-    for slab in range(slabs):
-        right = dot(inverse, whole_ref[:, slab, :])
-        right_ref[:, 128 * slab:128 * slab + 128] = right
-        total = total + right * right
+    right = stacked(inverse, jnp.concatenate([whole_ref[:, i, :] for i in range(slabs)], axis=1), 3)
+    right_ref[...] = right
+    total = sum(right[:, 128 * i:128 * i + 128] * right[:, 128 * i:128 * i + 128] for i in range(slabs))
     squares = dot(jnp.ones((8, 128), f32), total, ((1,), (1,)))
     squares = jnp.concatenate([squares, jnp.zeros((8, 128 - rank), f32)], axis=1)
     copies_ref[...] = jnp.broadcast_to(squares[None], copies_ref.shape)
@@ -109,15 +121,7 @@
     right = right_ref[...]
     ortho = ortho_ref[...]
     both = jnp.concatenate([(1.0 - decay_rate) * ortho, factor * (ortho * scale)], axis=0)
-    both_high = both.astype(jnp.bfloat16)
-    both_low = (both - both_high.astype(f32)).astype(jnp.bfloat16)
-    right_high = right.astype(jnp.bfloat16)
-    right_low = (right - right_high.astype(f32)).astype(jnp.bfloat16)
-    update = dot(
-        jnp.concatenate([both_high, both_low, both_high], axis=1),
-        jnp.concatenate([right_high, right_high, right_low], axis=0),
-        precision=lax.Precision.DEFAULT,
-    )
+    update = stacked(both, right, 2)
     new_momentum_ref[...] = buffer_ref[...] - update[:rows]
     new_weight_ref[...] = weight_ref[...] - update[rows:]
     new_basis_ref[...] = right * turned
@@ -130,6 +134,7 @@
         out_shape=[jax.ShapeDtypeStruct(shape, f32) for shape in shapes],
         in_specs=[in_vmem] * len(args),
         out_specs=[in_vmem] * len(shapes),
+        compiler_params=pltpu.CompilerParams(vmem_limit_bytes=16 * 2**20),
         name=name,
     )(*args)
 
@@ -138,9 +143,8 @@
     rank = right_basis.shape[1]
     rows, cols = weight.shape
     fsdp, tensor = lax.axis_size("fsdp"), lax.axis_size("tensor")
-    buffer, parts = call(
-        left_kernel, "left", (momentum, gradient, right_basis.T),
-        [(rows, cols), (tensor, rows // 2, 2 * rank)])
+    buffer = momentum + gradient.astype(f32)
+    (parts,) = call(left_kernel, "left", (buffer, right_basis.T), [(tensor, rows // 2, 2 * rank)])
     parts = exchange(parts, "tensor")
     left, products = call(product_kernel, "products", (parts, buffer), [(rows, rank), (rank, 8, 128)])
     mine = jnp.sum(exchange(products, "fsdp"), axis=0)

time: 102 us -> 93.9 us (0.921)
  Pallas kernels: 10.9 us -> 4.29 us
  blocking collectives: 89.7 us -> 87.5 us
  other arithmetic: 0.07 us -> 1.14 us
    pallas_call x4, Pallas kernels: 10.9 us -> 4.29 us  [call(): pl.pallas_call(kernel, out_shape=[jax.ShapeDtypeStruct(shape, f32) for sh...]
    all_to_all x4, blocking collectives: 89.7 us -> 87.5 us  [exchange(): return lax.all_to_all(blocks, axis, 0, 0)]
    add x0 -> x1, other arithmetic: none -> 1.07 us  [per_device(): buffer = momentum + gradient.astype(f32)]
where the time goes in v4:
time: 93.9 us; the launch traced here: 93.7 us
  blocking collectives  87.5 us (93%)
  Pallas kernels  4.29 us (5%)
  other arithmetic  1.14 us (1%)
    all_to_all x4, blocking collectives, exchange(): return lax.all_to_all(blocks, axis, 0, 0)  87.5 us
    pallas_call x4, Pallas kernels, call(): pl.pallas_call(kernel, out_shape=[jax.ShapeDtypeStruct(shape, f32) for sh...  4.29 us

profile of v4, /device:TPU:1, one launch (start us, length us, event | category | flops | bytes accessed | tf_op | source)
XLA Modules:
  0.0 93.7 jit_solution(15137902742721848478)
XLA Ops:
  0.6 0.0 copy-start
  0.6 1.1 %convert_add_fusion.buffer_ref = f32[64,896]{1,0:T(8,128)S(1)} fusion(f32[64,896]{1,0:T(8,128)} %param.5, bf16[64,896]{1,0:T(8,128)(2,1)} %param.6), kind=kLoop, calls=%fused_computation | loop fusion | flops 114688 | bytes 573440 | tf_op jit(solution)/shard_map/add | solution.py:146
  1.7 0.0 copy-done
  1.7 0.4 left.1
  2.2 29.7 %all_to_all.20.parts_ref = f32[16,32,128]{2,1,0:T(8,128)S(1)} all-to-all(f32[16,32,128]{2,1,0:T(8,128)S(1)} %left.1), channel_id=1, replica_groups=mesh['fsdp'=64,'tensor'=16] {'tensor'}, dimensions={0} | all-to-all | bytes 524288 | tf_op jit(solution)/shard_map/all_to_all | solution.py:19
  31.9 0.5 products.1
  32.4 27.0 %all_to_all.21 = f32[64,8,128]{2,1,0:T(8,128)S(1)} all-to-all(f32[64,8,128]{2,1,0:T(8,128)S(1)} %get-tuple-element.11), channel_id=1, replica_groups=mesh['fsdp'=64,'tensor'=16] {'fsdp'}, dimensions={0} | all-to-all | bytes 524288 | tf_op jit(solution)/shard_map/all_to_all | solution.py:19
  59.3 0.1 reduce_sum.9
  59.4 17.2 %all_to_all.22.whole_ref = f32[64,8,128]{2,1,0:T(8,128)S(1)} all-to-all(f32[64,8,128]{2,1,0:T(8,128)S(1)} %broadcast_in_dim.2), channel_id=1, replica_groups=mesh['fsdp'=64,'tensor'=16] {'fsdp'}, dimensions={0} | all-to-all | bytes 524288 | tf_op jit(solution)/shard_map/all_to_all | solution.py:19
  76.7 0.0 copy-start.1
  76.7 2.3 %factor.1 = (f32[64,896]{1,0:T(8,128)S(1)}, f32[64,64]{1,0:T(8,128)S(1)}, f32[16,8,128]{2,1,0:T(8,128)S(1)}) custom-call(f32[64,8,128]{2,1,0:T(8,128)S(1)} %all_to_all.22.whole_ref, f32[64,64]{1,0:T(8,128)S(1)} %get-tuple-element.12.left_ref), custom_call_target="tpu_custom_call" | custom-call | tf_op jit(solution)/shard_map/factor/pallas_call | solution.py:132
  79.0 13.6 %all_to_all.23.squares_ref = f32[16,8,128]{2,1,0:T(8,128)S(1)} all-to-all(f32[16,8,128]{2,1,0:T(8,128)S(1)} %get-tuple-element.13), channel_id=1, replica_groups=mesh['fsdp'=64,'tensor'=16] {'tensor'}, dimensions={0} | all-to-all | bytes 131072 | tf_op jit(solution)/shard_map/all_to_all | solution.py:19
  92.6 0.0 copy-done.1
  92.6 1.1 %update.1 = (f32[64,896]{1,0:T(8,128)}, f32[64,896]{1,0:T(8,128)}, f32[64,896]{1,0:T(8,128)}) custom-call(f32[16,8,128]{2,1,0:T(8,128)S(1)} %all_to_all.23.squares_ref, f32[64,896]{1,0:T(8,128)S(1)} %get-tuple-element.14.right_ref, f32[64,64]{1,0:T(8,128)S(1)} %get-tuple-element.15.ortho_ref, f32[64,896]{1,0:T(8,128)S(1)} %convert_add_fusion.buffer_ref, ...), custom_call_target="tpu_custom_call" | custom-call | tf_op jit(solution)/shard_map/update/pallas_call | solution.py:132
  (1 shorter events, 0.0 us)
Async XLA Ops:
  0.6 1.1 %copy-start = (f32[896,64]{0,1:T(8,128)S(1)}, f32[896,64]{0,1:T(8,128)}, u32[]{:S(2)}) copy-start(f32[896,64]{0,1:T(8,128)} %param.7) | copy-start | bytes 688132
  76.7 15.9 %copy-start.1 = (f32[64,896]{1,0:T(8,128)S(1)}, f32[64,896]{1,0:T(8,128)}, u32[]{:S(2)}) copy-start(f32[64,896]{1,0:T(8,128)} %weight_ref.1) | copy-start | bytes 688132

commit v5 on v4

--- a/solution.py
+++ b/solution.py
@@ -15,12 +15,22 @@
 f32 = jnp.float32
 
 
-def exchange(blocks, axis):
-    return lax.all_to_all(blocks, axis, 0, 0)
+def exchange(blocks, axis, groups=None):
+    return lax.all_to_all(blocks, axis, 0, 0, axis_index_groups=groups)
 
 
-def copies(block, axis):
-    return jnp.broadcast_to(block[None], (lax.axis_size(axis),) + block.shape)
+def copies(block, count):
+    return jnp.broadcast_to(block[None], (count,) + block.shape)
+
+
+def sum_over_fsdp(blocks):
+    side = math.isqrt(lax.axis_size("fsdp"))
+    lines = [[side * i + j for j in range(side)] for i in range(side)]
+    across = [list(line) for line in zip(*lines)]
+    parts = blocks.reshape(side, -1, blocks.shape[-1])
+    mine = jnp.sum(exchange(parts, "fsdp", lines), axis=0)
+    mine = jnp.sum(exchange(copies(mine, side), "fsdp", across), axis=0)
+    return exchange(copies(mine, side), "fsdp", lines).reshape(blocks.shape)
 
 
 def eliminate(blocks, size, width):
@@ -147,8 +157,7 @@
     (parts,) = call(left_kernel, "left", (buffer, right_basis.T), [(tensor, rows // 2, 2 * rank)])
     parts = exchange(parts, "tensor")
     left, products = call(product_kernel, "products", (parts, buffer), [(rows, rank), (rank, 8, 128)])
-    mine = jnp.sum(exchange(products, "fsdp"), axis=0)
-    whole = exchange(copies(mine, "fsdp"), "fsdp")
+    whole = sum_over_fsdp(products)
     right, ortho, squares = call(
         factor_kernel, "factor", (whole, left),
         [(rank, cols), (rows, rank), (tensor, 8, 128)])

time: 93.9 us -> 98.2 us (1.046)
  blocking collectives: 87.5 us -> 91.8 us
    all_to_all x4 -> x5, blocking collectives: 87.5 us -> 91.8 us  [exchange(): return lax.all_to_all(blocks, axis, 0, 0, axis_index_groups=groups)]
where the time goes in v5:
time: 98.2 us; the launch traced here: 97.9 us
  blocking collectives  91.8 us (93%)
  Pallas kernels  4.29 us (4%)
  other arithmetic  1.11 us (1%)
    all_to_all x5, blocking collectives, exchange(): return lax.all_to_all(blocks, axis, 0, 0, axis_index_groups=groups)  91.8 us
    pallas_call x4, Pallas kernels, call(): pl.pallas_call(kernel, out_shape=[jax.ShapeDtypeStruct(shape, f32) for sh...  4.29 us

profile of v5, /device:TPU:1, one launch (start us, length us, event | category | flops | bytes accessed | tf_op | source)
XLA Modules:
  0.0 97.9 jit_solution(18341693567032751529)
XLA Ops:
  0.6 0.0 copy-start
  0.6 1.1 %convert_add_fusion.buffer_ref = f32[64,896]{1,0:T(8,128)S(1)} fusion(f32[64,896]{1,0:T(8,128)} %param.5, bf16[64,896]{1,0:T(8,128)(2,1)} %param.6), kind=kLoop, calls=%fused_computation | loop fusion | flops 114688 | bytes 573440 | tf_op jit(solution)/shard_map/add | solution.py:156
  1.7 0.0 copy-done
  1.7 0.4 left.1
  2.2 29.7 %all_to_all.25.parts_ref = f32[16,32,128]{2,1,0:T(8,128)S(1)} all-to-all(f32[16,32,128]{2,1,0:T(8,128)S(1)} %left.1), channel_id=1, replica_groups=mesh['fsdp'=64,'tensor'=16] {'tensor'}, dimensions={0} | all-to-all | bytes 524288 | tf_op jit(solution)/shard_map/all_to_all | solution.py:19
  31.9 0.5 products.1
  32.4 18.7 %all_to_all.26 = f32[8,64,128]{2,1,0:T(8,128)S(1)} all-to-all(f32[8,64,128]{2,1,0:T(8,128)S(1)} %bitcast.5), channel_id=1, replica_groups={{0,16,32,48,64,80,96,112},{128,144,160,176,192,208,224,240},{256,272,28..., dimensions={0} | all-to-all | bytes 524288 | tf_op jit(solution)/shard_map/all_to_all | solution.py:19
  51.1 17.9 %all_to_all.27 = f32[8,64,128]{2,1,0:T(8,128)S(1)} all-to-all(f32[8,64,128]{2,1,0:T(8,128)S(1)} %broadcast_in_dim.4), channel_id=1, replica_groups={{0,128,256,384,512,640,768,896},{16,144,272,400,528,656,784,912},{32,16..., dimensions={0} | all-to-all | bytes 524288 | tf_op jit(solution)/shard_map/all_to_all | solution.py:19
  69.0 11.6 %all_to_all.28 = f32[8,64,128]{2,1,0:T(8,128)S(1)} all-to-all(f32[8,64,128]{2,1,0:T(8,128)S(1)} %broadcast_in_dim.5), channel_id=1, replica_groups={{0,16,32,48,64,80,96,112},{128,144,160,176,192,208,224,240},{256,272,28..., dimensions={0} | all-to-all | bytes 524288 | tf_op jit(solution)/shard_map/all_to_all | solution.py:19
  80.6 0.0 copy-start.1
  80.6 2.3 %factor.1 = (f32[64,896]{1,0:T(8,128)S(1)}, f32[64,64]{1,0:T(8,128)S(1)}, f32[16,8,128]{2,1,0:T(8,128)S(1)}) custom-call(f32[64,8,128]{2,1,0:T(8,128)S(1)} %bitcast.4, f32[64,64]{1,0:T(8,128)S(1)} %get-tuple-element.12.left_ref), custom_call_target="tpu_custom_call" | custom-call | tf_op jit(solution)/shard_map/factor/pallas_call | solution.py:142
  82.9 13.9 %all_to_all.29.squares_ref = f32[16,8,128]{2,1,0:T(8,128)S(1)} all-to-all(f32[16,8,128]{2,1,0:T(8,128)S(1)} %get-tuple-element.13), channel_id=1, replica_groups=mesh['fsdp'=64,'tensor'=16] {'tensor'}, dimensions={0} | all-to-all | bytes 131072 | tf_op jit(solution)/shard_map/all_to_all | solution.py:19
  96.8 0.0 copy-done.1
  96.8 1.1 %update.1 = (f32[64,896]{1,0:T(8,128)}, f32[64,896]{1,0:T(8,128)}, f32[64,896]{1,0:T(8,128)}) custom-call(f32[16,8,128]{2,1,0:T(8,128)S(1)} %all_to_all.29.squares_ref, f32[64,896]{1,0:T(8,128)S(1)} %get-tuple-element.14.right_ref, f32[64,64]{1,0:T(8,128)S(1)} %get-tuple-element.15.ortho_ref, f32[64,896]{1,0:T(8,128)S(1)} %convert_add_fusion.buffer_ref, ...), custom_call_target="tpu_custom_call" | custom-call | tf_op jit(solution)/shard_map/update/pallas_call | solution.py:142
  (4 shorter events, 0.1 us)
Async XLA Ops:
  0.6 1.1 %copy-start = (f32[896,64]{0,1:T(8,128)S(1)}, f32[896,64]{0,1:T(8,128)}, u32[]{:S(2)}) copy-start(f32[896,64]{0,1:T(8,128)} %param.7) | copy-start | bytes 688132
  80.6 16.2 %copy-start.1 = (f32[64,896]{1,0:T(8,128)S(1)}, f32[64,896]{1,0:T(8,128)}, u32[]{:S(2)}) copy-start(f32[64,896]{1,0:T(8,128)} %weight_ref.1) | copy-start | bytes 688132

commit v6 on v4

--- a/solution.py
+++ b/solution.py
@@ -16,7 +16,16 @@
 
 
 def exchange(blocks, axis):
-    return lax.all_to_all(blocks, axis, 0, 0)
+    return lax.all_to_all(blocks, axis, 0, 0, axis_index_groups=[order(axis)])
+
+
+def order(axis):
+    count = lax.axis_size(axis)
+    if axis == "tensor":
+        return list(range(count))[::-1]
+    side = math.isqrt(count)
+    turned = [(i + 4) % side for i in range(side)]
+    return [side * y + x for y in turned for x in turned]
 
 
 def copies(block, axis):

time: 93.9 us -> 84.1 us (0.90)
  blocking collectives: 87.5 us -> 77.7 us
    all_to_all x4, blocking collectives: 87.5 us -> 77.7 us  [exchange(): return lax.all_to_all(blocks, axis, 0, 0, axis_index_groups=[order(axis)])]
where the time goes in v6:
time: 84.1 us; the launch traced here: 83.9 us
  blocking collectives  77.7 us (92%)
  Pallas kernels  4.29 us (5%)
  other arithmetic  1.14 us (1%)
    all_to_all x4, blocking collectives, exchange(): return lax.all_to_all(blocks, axis, 0, 0, axis_index_groups=[order(axis)])  77.7 us
    pallas_call x4, Pallas kernels, call(): pl.pallas_call(kernel, out_shape=[jax.ShapeDtypeStruct(shape, f32) for sh...  4.29 us

profile of v6, /device:TPU:1, one launch (start us, length us, event | category | flops | bytes accessed | tf_op | source)
XLA Modules:
  0.0 83.9 jit_solution(8977125648773994351)
XLA Ops:
  0.6 0.0 copy-start
  0.6 1.1 %convert_add_fusion.buffer_ref = f32[64,896]{1,0:T(8,128)S(1)} fusion(f32[64,896]{1,0:T(8,128)} %param.5, bf16[64,896]{1,0:T(8,128)(2,1)} %param.6), kind=kLoop, calls=%fused_computation | loop fusion | flops 114688 | bytes 573440 | tf_op jit(solution)/shard_map/add | solution.py:155
  1.7 0.0 copy-done
  1.7 0.4 left.1
  2.2 26.9 %all_to_all.20.parts_ref = f32[16,32,128]{2,1,0:T(8,128)S(1)} all-to-all(f32[16,32,128]{2,1,0:T(8,128)S(1)} %left.1), channel_id=1, replica_groups={{15,14,13,12,11,10,9,8,7,6,5,4,3,2,1,0},{31,30,29,28,27,26,25,24,23,22,..., dimensions={0} | all-to-all | bytes 524288 | tf_op jit(solution)/shard_map/all_to_all | solution.py:19
  29.1 0.5 products.1
  29.5 21.0 %all_to_all.21 = f32[64,8,128]{2,1,0:T(8,128)S(1)} all-to-all(f32[64,8,128]{2,1,0:T(8,128)S(1)} %get-tuple-element.11), channel_id=1, replica_groups={{576,592,608,624,512,528,544,560,704,720,736,752,640,656,672,688,832,84..., dimensions={0} | all-to-all | bytes 524288 | tf_op jit(solution)/shard_map/all_to_all | solution.py:19
  50.5 0.1 reduce_sum.9
  50.6 17.7 %all_to_all.22.whole_ref = f32[64,8,128]{2,1,0:T(8,128)S(1)} all-to-all(f32[64,8,128]{2,1,0:T(8,128)S(1)} %broadcast_in_dim.2), channel_id=1, replica_groups={{576,592,608,624,512,528,544,560,704,720,736,752,640,656,672,688,832,84..., dimensions={0} | all-to-all | bytes 524288 | tf_op jit(solution)/shard_map/all_to_all | solution.py:19
  68.3 0.0 copy-start.1
  68.3 2.3 %factor.1 = (f32[64,896]{1,0:T(8,128)S(1)}, f32[64,64]{1,0:T(8,128)S(1)}, f32[16,8,128]{2,1,0:T(8,128)S(1)}) custom-call(f32[64,8,128]{2,1,0:T(8,128)S(1)} %all_to_all.22.whole_ref, f32[64,64]{1,0:T(8,128)S(1)} %get-tuple-element.12.left_ref), custom_call_target="tpu_custom_call" | custom-call | tf_op jit(solution)/shard_map/factor/pallas_call | solution.py:141
  70.6 12.1 %all_to_all.23.squares_ref = f32[16,8,128]{2,1,0:T(8,128)S(1)} all-to-all(f32[16,8,128]{2,1,0:T(8,128)S(1)} %get-tuple-element.13), channel_id=1, replica_groups={{15,14,13,12,11,10,9,8,7,6,5,4,3,2,1,0},{31,30,29,28,27,26,25,24,23,22,..., dimensions={0} | all-to-all | bytes 131072 | tf_op jit(solution)/shard_map/all_to_all | solution.py:19
  82.8 0.0 copy-done.1
  82.8 1.1 %update.1 = (f32[64,896]{1,0:T(8,128)}, f32[64,896]{1,0:T(8,128)}, f32[64,896]{1,0:T(8,128)}) custom-call(f32[16,8,128]{2,1,0:T(8,128)S(1)} %all_to_all.23.squares_ref, f32[64,896]{1,0:T(8,128)S(1)} %get-tuple-element.14.right_ref, f32[64,64]{1,0:T(8,128)S(1)} %get-tuple-element.15.ortho_ref, f32[64,896]{1,0:T(8,128)S(1)} %convert_add_fusion.buffer_ref, ...), custom_call_target="tpu_custom_call" | custom-call | tf_op jit(solution)/shard_map/update/pallas_call | solution.py:141
  (1 shorter events, 0.0 us)
Async XLA Ops:
  0.6 1.1 %copy-start = (f32[896,64]{0,1:T(8,128)S(1)}, f32[896,64]{0,1:T(8,128)}, u32[]{:S(2)}) copy-start(f32[896,64]{0,1:T(8,128)} %param.7) | copy-start | bytes 688132
  68.3 14.4 %copy-start.1 = (f32[64,896]{1,0:T(8,128)S(1)}, f32[64,896]{1,0:T(8,128)}, u32[]{:S(2)}) copy-start(f32[64,896]{1,0:T(8,128)} %weight_ref.1) | copy-start | bytes 688132

commit v7 on v6

--- a/solution.py
+++ b/solution.py
@@ -49,14 +49,15 @@
             inverse = 1.0 / spread_row(columns[k][first], k)
             row = spread_row(blocks[first], k)
             ratio = {i: columns[k][i] * inverse for i in live}
-            ratio[first] = jnp.where(sublane > k, ratio[first], 0.0)
+            below = jnp.where(sublane > k, ratio[first], 0.0)
             for later in range(k + 1, 8):
                 entry = spread_row(columns[later][first], k)
                 for i in live:
                     columns[later][i] = columns[later][i] - ratio[i] * entry
-            for i in live:
-                if i > first or k < 7:
-                    blocks[i] = blocks[i] - ratio[i] * row
+            if k < 7:
+                blocks[first] = blocks[first] - below * row
+            for i in range(first + 1, count):
+                blocks[i] = blocks[i] - ratio[i] * row
     return blocks
 
 
@@ -113,8 +114,8 @@
     right = stacked(inverse, jnp.concatenate([whole_ref[:, i, :] for i in range(slabs)], axis=1), 3)
     right_ref[...] = right
     total = sum(right[:, 128 * i:128 * i + 128] * right[:, 128 * i:128 * i + 128] for i in range(slabs))
-    squares = dot(jnp.ones((8, 128), f32), total, ((1,), (1,)))
-    squares = jnp.concatenate([squares, jnp.zeros((8, 128 - rank), f32)], axis=1)
+    squares = dot(jnp.ones((8, 128), f32), total, ((1,), (1,)))[:1]
+    squares = jnp.concatenate([squares, jnp.zeros((1, 128 - rank), f32)], axis=1)
     copies_ref[...] = jnp.broadcast_to(squares[None], copies_ref.shape)
     ortho_ref[...] = dot(left_ref[...], inverse, ((1,), (1,)))
 
@@ -122,7 +123,7 @@
 def update_kernel(factor, squares_ref, right_ref, ortho_ref, buffer_ref, weight_ref,
                   new_weight_ref, new_momentum_ref, new_basis_ref):
     rows, rank = ortho_ref.shape
-    norms = jnp.sqrt(jnp.sum(squares_ref[...], axis=0))[:1, :rank]
+    norms = jnp.sqrt(jnp.sum(squares_ref[...], axis=0))[:, :rank]
     scale = 1.0 / (norms + tiny_eps)
     row = lax.broadcasted_iota(jnp.int32, (rank, rank), 0)
     column = lax.broadcasted_iota(jnp.int32, (rank, rank), 1)
@@ -160,7 +161,7 @@
     whole = exchange(copies(mine, "fsdp"), "fsdp")
     right, ortho, squares = call(
         factor_kernel, "factor", (whole, left),
-        [(rank, cols), (rows, rank), (tensor, 8, 128)])
+        [(rank, cols), (rows, rank), (tensor, 1, 128)])
     squares = exchange(squares, "tensor")
     factor = step_size * math.sqrt(rows * fsdp * cols * tensor / rank)
     new_weight, new_momentum, new_basis = call(

time: 84.1 us -> 83.4 us (level)
  no operation moved by 1% of the time
where the time goes in v7:
time: 83.4 us; the launch traced here: 83.1 us
  blocking collectives  77 us (92%)
  Pallas kernels  4.25 us (5%)
  other arithmetic  1.14 us (1%)
    all_to_all x4, blocking collectives, exchange(): return lax.all_to_all(blocks, axis, 0, 0, axis_index_groups=[order(axis)])  77 us
    pallas_call x4, Pallas kernels, call(): pl.pallas_call(kernel, out_shape=[jax.ShapeDtypeStruct(shape, f32) for sh...  4.25 us

profile of v7, /device:TPU:1, one launch (start us, length us, event | category | flops | bytes accessed | tf_op | source)
XLA Modules:
  0.0 83.1 jit_solution(11758290207729694203)
XLA Ops:
  0.6 0.0 copy-start
  0.6 1.1 %convert_add_fusion.buffer_ref = f32[64,896]{1,0:T(8,128)S(1)} fusion(f32[64,896]{1,0:T(8,128)} %param.5, bf16[64,896]{1,0:T(8,128)(2,1)} %param.6), kind=kLoop, calls=%fused_computation | loop fusion | flops 114688 | bytes 573440 | tf_op jit(solution)/shard_map/add | solution.py:156
  1.7 0.0 copy-done
  1.7 0.4 left.1
  2.2 26.9 %all_to_all.20.parts_ref = f32[16,32,128]{2,1,0:T(8,128)S(1)} all-to-all(f32[16,32,128]{2,1,0:T(8,128)S(1)} %left.1), channel_id=1, replica_groups={{15,14,13,12,11,10,9,8,7,6,5,4,3,2,1,0},{31,30,29,28,27,26,25,24,23,22,..., dimensions={0} | all-to-all | bytes 524288 | tf_op jit(solution)/shard_map/all_to_all | solution.py:19
  29.1 0.5 products.1
  29.5 21.0 %all_to_all.21 = f32[64,8,128]{2,1,0:T(8,128)S(1)} all-to-all(f32[64,8,128]{2,1,0:T(8,128)S(1)} %get-tuple-element.11), channel_id=1, replica_groups={{576,592,608,624,512,528,544,560,704,720,736,752,640,656,672,688,832,84..., dimensions={0} | all-to-all | bytes 524288 | tf_op jit(solution)/shard_map/all_to_all | solution.py:19
  50.5 0.1 reduce_sum.9
  50.6 17.7 %all_to_all.22.whole_ref = f32[64,8,128]{2,1,0:T(8,128)S(1)} all-to-all(f32[64,8,128]{2,1,0:T(8,128)S(1)} %broadcast_in_dim.2), channel_id=1, replica_groups={{576,592,608,624,512,528,544,560,704,720,736,752,640,656,672,688,832,84..., dimensions={0} | all-to-all | bytes 524288 | tf_op jit(solution)/shard_map/all_to_all | solution.py:19
  68.3 0.0 copy-start.1
  68.3 2.3 %factor.1 = (f32[64,896]{1,0:T(8,128)S(1)}, f32[64,64]{1,0:T(8,128)S(1)}, f32[16,1,128]{2,1,0:T(1,128)S(1)}) custom-call(f32[64,8,128]{2,1,0:T(8,128)S(1)} %all_to_all.22.whole_ref, f32[64,64]{1,0:T(8,128)S(1)} %get-tuple-element.12.left_ref), custom_call_target="tpu_custom_call" | custom-call | tf_op jit(solution)/shard_map/factor/pallas_call | solution.py:142
  70.6 11.4 %all_to_all.23.squares_ref = f32[16,1,128]{2,1,0:T(1,128)S(1)} all-to-all(f32[16,1,128]{2,1,0:T(1,128)S(1)} %get-tuple-element.13), channel_id=1, replica_groups={{15,14,13,12,11,10,9,8,7,6,5,4,3,2,1,0},{31,30,29,28,27,26,25,24,23,22,..., dimensions={0} | all-to-all | bytes 16384 | tf_op jit(solution)/shard_map/all_to_all | solution.py:19
  82.0 0.0 copy-done.1
  82.0 1.1 %update.1 = (f32[64,896]{1,0:T(8,128)}, f32[64,896]{1,0:T(8,128)}, f32[64,896]{1,0:T(8,128)}) custom-call(f32[16,1,128]{2,1,0:T(1,128)S(1)} %all_to_all.23.squares_ref, f32[64,896]{1,0:T(8,128)S(1)} %get-tuple-element.14.right_ref, f32[64,64]{1,0:T(8,128)S(1)} %get-tuple-element.15.ortho_ref, f32[64,896]{1,0:T(8,128)S(1)} %convert_add_fusion.buffer_ref, ...), custom_call_target="tpu_custom_call" | custom-call | tf_op jit(solution)/shard_map/update/pallas_call | solution.py:142
  (1 shorter events, 0.0 us)
Async XLA Ops:
  0.6 1.1 %copy-start = (f32[896,64]{0,1:T(8,128)S(1)}, f32[896,64]{0,1:T(8,128)}, u32[]{:S(2)}) copy-start(f32[896,64]{0,1:T(8,128)} %param.7) | copy-start | bytes 688132
  68.3 13.7 %copy-start.1 = (f32[64,896]{1,0:T(8,128)S(1)}, f32[64,896]{1,0:T(8,128)}, u32[]{:S(2)}) copy-start(f32[64,896]{1,0:T(8,128)} %weight_ref.1) | copy-start | bytes 688132

commit v8 on v7

--- a/solution.py
+++ b/solution.py
@@ -22,7 +22,9 @@
 def order(axis):
     count = lax.axis_size(axis)
     if axis == "tensor":
-        return list(range(count))[::-1]
+        planes = count // 2
+        others = sorted(range(planes - 1), key=lambda z: (min(z, planes - z), -z))
+        return [2 * z + core for z in [planes - 1] + others for core in (1, 0)]
     side = math.isqrt(count)
     turned = [(i + 4) % side for i in range(side)]
     return [side * y + x for y in turned for x in turned]

time: 83.4 us -> 83.3 us (level)
  no operation moved by 1% of the time
where the time goes in v8:
time: 83.3 us; the launch traced here: 83 us
  blocking collectives  76.9 us (92%)
  Pallas kernels  4.25 us (5%)
  other arithmetic  1.14 us (1%)
    all_to_all x4, blocking collectives, exchange(): return lax.all_to_all(blocks, axis, 0, 0, axis_index_groups=[order(axis)])  76.9 us
    pallas_call x4, Pallas kernels, call(): pl.pallas_call(kernel, out_shape=[jax.ShapeDtypeStruct(shape, f32) for sh...  4.25 us

profile of v8, /device:TPU:1, one launch (start us, length us, event | category | flops | bytes accessed | tf_op | source)
XLA Modules:
  0.0 83.0 jit_solution(13364024244675306441)
XLA Ops:
  0.6 0.0 copy-start
  0.6 1.1 %convert_add_fusion.buffer_ref = f32[64,896]{1,0:T(8,128)S(1)} fusion(f32[64,896]{1,0:T(8,128)} %param.5, bf16[64,896]{1,0:T(8,128)(2,1)} %param.6), kind=kLoop, calls=%fused_computation | loop fusion | flops 114688 | bytes 573440 | tf_op jit(solution)/shard_map/add | solution.py:158
  1.7 0.0 copy-done
  1.7 0.4 left.1
  2.2 27.3 %all_to_all.20.parts_ref = f32[16,32,128]{2,1,0:T(8,128)S(1)} all-to-all(f32[16,32,128]{2,1,0:T(8,128)S(1)} %left.1), channel_id=1, replica_groups={{15,14,1,0,3,2,13,12,5,4,11,10,7,6,9,8},{31,30,17,16,19,18,29,28,21,20,..., dimensions={0} | all-to-all | bytes 524288 | tf_op jit(solution)/shard_map/all_to_all | solution.py:19
  29.5 0.5 products.1
  30.0 20.8 %all_to_all.21 = f32[64,8,128]{2,1,0:T(8,128)S(1)} all-to-all(f32[64,8,128]{2,1,0:T(8,128)S(1)} %get-tuple-element.11), channel_id=1, replica_groups={{576,592,608,624,512,528,544,560,704,720,736,752,640,656,672,688,832,84..., dimensions={0} | all-to-all | bytes 524288 | tf_op jit(solution)/shard_map/all_to_all | solution.py:19
  50.8 0.1 reduce_sum.9
  50.9 17.7 %all_to_all.22.whole_ref = f32[64,8,128]{2,1,0:T(8,128)S(1)} all-to-all(f32[64,8,128]{2,1,0:T(8,128)S(1)} %broadcast_in_dim.2), channel_id=1, replica_groups={{576,592,608,624,512,528,544,560,704,720,736,752,640,656,672,688,832,84..., dimensions={0} | all-to-all | bytes 524288 | tf_op jit(solution)/shard_map/all_to_all | solution.py:19
  68.6 0.0 copy-start.1
  68.6 2.2 %factor.1 = (f32[64,896]{1,0:T(8,128)S(1)}, f32[64,64]{1,0:T(8,128)S(1)}, f32[16,1,128]{2,1,0:T(1,128)S(1)}) custom-call(f32[64,8,128]{2,1,0:T(8,128)S(1)} %all_to_all.22.whole_ref, f32[64,64]{1,0:T(8,128)S(1)} %get-tuple-element.12.left_ref), custom_call_target="tpu_custom_call" | custom-call | tf_op jit(solution)/shard_map/factor/pallas_call | solution.py:144
  70.8 11.0 %all_to_all.23.squares_ref = f32[16,1,128]{2,1,0:T(1,128)S(1)} all-to-all(f32[16,1,128]{2,1,0:T(1,128)S(1)} %get-tuple-element.13), channel_id=1, replica_groups={{15,14,1,0,3,2,13,12,5,4,11,10,7,6,9,8},{31,30,17,16,19,18,29,28,21,20,..., dimensions={0} | all-to-all | bytes 16384 | tf_op jit(solution)/shard_map/all_to_all | solution.py:19
  81.9 0.0 copy-done.1
  81.9 1.1 %update.1 = (f32[64,896]{1,0:T(8,128)}, f32[64,896]{1,0:T(8,128)}, f32[64,896]{1,0:T(8,128)}) custom-call(f32[16,1,128]{2,1,0:T(1,128)S(1)} %all_to_all.23.squares_ref, f32[64,896]{1,0:T(8,128)S(1)} %get-tuple-element.14.right_ref, f32[64,64]{1,0:T(8,128)S(1)} %get-tuple-element.15.ortho_ref, f32[64,896]{1,0:T(8,128)S(1)} %convert_add_fusion.buffer_ref, ...), custom_call_target="tpu_custom_call" | custom-call | tf_op jit(solution)/shard_map/update/pallas_call | solution.py:144
  (1 shorter events, 0.0 us)
Async XLA Ops:
  0.6 1.1 %copy-start = (f32[896,64]{0,1:T(8,128)S(1)}, f32[896,64]{0,1:T(8,128)}, u32[]{:S(2)}) copy-start(f32[896,64]{0,1:T(8,128)} %param.7) | copy-start | bytes 688132
  68.6 13.3 %copy-start.1 = (f32[64,896]{1,0:T(8,128)S(1)}, f32[64,896]{1,0:T(8,128)}, u32[]{:S(2)}) copy-start(f32[64,896]{1,0:T(8,128)} %weight_ref.1) | copy-start | bytes 688132

commit v9 on v8

--- a/solution.py
+++ b/solution.py
@@ -122,20 +122,19 @@
     ortho_ref[...] = dot(left_ref[...], inverse, ((1,), (1,)))
 
 
-def update_kernel(factor, squares_ref, right_ref, ortho_ref, buffer_ref, weight_ref,
-                  new_weight_ref, new_momentum_ref, new_basis_ref):
-    rows, rank = ortho_ref.shape
+def momentum_kernel(right_ref, ortho_ref, buffer_ref, new_momentum_ref):
+    new_momentum_ref[...] = buffer_ref[...] - stacked((1.0 - decay_rate) * ortho_ref[...], right_ref[...], 2)
+
+
+def weight_kernel(factor, squares_ref, right_ref, ortho_ref, weight_ref, new_weight_ref, new_basis_ref):
+    rank = ortho_ref.shape[1]
     norms = jnp.sqrt(jnp.sum(squares_ref[...], axis=0))[:, :rank]
     scale = 1.0 / (norms + tiny_eps)
     row = lax.broadcasted_iota(jnp.int32, (rank, rank), 0)
     column = lax.broadcasted_iota(jnp.int32, (rank, rank), 1)
     turned = jnp.sum(jnp.where(row == column, scale, 0.0), axis=1, keepdims=True)
     right = right_ref[...]
-    ortho = ortho_ref[...]
-    both = jnp.concatenate([(1.0 - decay_rate) * ortho, factor * (ortho * scale)], axis=0)
-    update = stacked(both, right, 2)
-    new_momentum_ref[...] = buffer_ref[...] - update[:rows]
-    new_weight_ref[...] = weight_ref[...] - update[rows:]
+    new_weight_ref[...] = weight_ref[...] - stacked(factor * (ortho_ref[...] * scale), right, 2)
     new_basis_ref[...] = right * turned
 
 
@@ -166,9 +165,10 @@
         [(rank, cols), (rows, rank), (tensor, 1, 128)])
     squares = exchange(squares, "tensor")
     factor = step_size * math.sqrt(rows * fsdp * cols * tensor / rank)
-    new_weight, new_momentum, new_basis = call(
-        functools.partial(update_kernel, factor), "update", (squares, right, ortho, buffer, weight),
-        [(rows, cols), (rows, cols), (rank, cols)])
+    (new_momentum,) = call(momentum_kernel, "momentum", (right, ortho, buffer), [(rows, cols)])
+    new_weight, new_basis = call(
+        functools.partial(weight_kernel, factor), "weight", (squares, right, ortho, weight),
+        [(rows, cols), (rank, cols)])
     return (new_weight, new_momentum, new_basis.T)
 
 

time: 83.3 us -> 83.9 us (level)
  blocking collectives: 76.9 us -> 65.8 us
  starting transfers between devices: 0 us -> 6.48 us
  waiting for transfers between devices: 0 us -> 3.75 us
  Pallas kernels: 4.25 us -> 5.66 us
    all_to_all x4 -> x3, blocking collectives: 76.9 us -> 65.8 us  [exchange(): return lax.all_to_all(blocks, axis, 0, 0, axis_index_groups=[order(axis)])]
    all_to_all x0 -> x1, starting transfers between devices: none -> 6.48 us  [exchange(): return lax.all_to_all(blocks, axis, 0, 0, axis_index_groups=[order(axis)])]
    all_to_all x0 -> x1, waiting for transfers between devices: none -> 3.75 us  [exchange(): return lax.all_to_all(blocks, axis, 0, 0, axis_index_groups=[order(axis)])]
    pallas_call x4 -> x5, Pallas kernels: 4.25 us -> 5.66 us  [call(): pl.pallas_call(kernel, out_shape=[jax.ShapeDtypeStruct(shape, f32) for sh...]
  transfers between devices with their start and end apart: 0 -> 1, of which waited for: 0 -> 1; matrix products, arithmetic and copies ran while one was open for 0% -> 0% of each run, Pallas kernels for 0% -> 1%
where the time goes in v9:
time: 83.9 us; the launch traced here: 83.6 us
  blocking collectives  65.8 us (78%)
  starting transfers between devices  6.48 us (8%)
  Pallas kernels  5.66 us (7%)
  waiting for transfers between devices  3.75 us (4%)
  other arithmetic  1.14 us (1%)
    all_to_all x3, blocking collectives, exchange(): return lax.all_to_all(blocks, axis, 0, 0, axis_index_groups=[order(axis)])  65.8 us
    all_to_all x1, starting transfers between devices, exchange(): return lax.all_to_all(blocks, axis, 0, 0, axis_index_groups=[order(axis)])  6.48 us
    pallas_call x5, Pallas kernels, call(): pl.pallas_call(kernel, out_shape=[jax.ShapeDtypeStruct(shape, f32) for sh...  5.66 us
    all_to_all x1, waiting for transfers between devices, exchange(): return lax.all_to_all(blocks, axis, 0, 0, axis_index_groups=[order(axis)])  3.75 us
  transfers between devices with their start and end apart: 1, of which 1 were waited for; matrix products, arithmetic and copies ran while one was open for 0% of the time, Pallas kernels for 1%

profile of v9, /device:TPU:1, one launch (start us, length us, event | category | flops | bytes accessed | tf_op | source)
XLA Modules:
  0.0 83.6 jit_solution(892882349433726934)
XLA Ops:
  0.6 0.0 copy-start
  0.6 1.1 %convert_add_fusion.buffer_ref = f32[64,896]{1,0:T(8,128)S(1)} fusion(f32[64,896]{1,0:T(8,128)} %param.5, bf16[64,896]{1,0:T(8,128)(2,1)} %param.6), kind=kLoop, calls=%fused_computation | loop fusion | flops 114688 | bytes 573440 | tf_op jit(solution)/shard_map/add | solution.py:157
  1.7 0.0 copy-done
  1.7 0.4 left.1
  2.2 27.3 %all_to_all.20.parts_ref = f32[16,32,128]{2,1,0:T(8,128)S(1)} all-to-all(f32[16,32,128]{2,1,0:T(8,128)S(1)} %left.1), channel_id=1, replica_groups={{15,14,1,0,3,2,13,12,5,4,11,10,7,6,9,8},{31,30,17,16,19,18,29,28,21,20,..., dimensions={0} | all-to-all | bytes 524288 | tf_op jit(solution)/shard_map/all_to_all | solution.py:19
  29.5 0.5 products.1
  30.0 20.8 %all_to_all.21 = f32[64,8,128]{2,1,0:T(8,128)S(1)} all-to-all(f32[64,8,128]{2,1,0:T(8,128)S(1)} %get-tuple-element.10), channel_id=1, replica_groups={{576,592,608,624,512,528,544,560,704,720,736,752,640,656,672,688,832,84..., dimensions={0} | all-to-all | bytes 524288 | tf_op jit(solution)/shard_map/all_to_all | solution.py:19
  50.8 0.1 reduce_sum.9
  50.9 17.7 %all_to_all.22.whole_ref = f32[64,8,128]{2,1,0:T(8,128)S(1)} all-to-all(f32[64,8,128]{2,1,0:T(8,128)S(1)} %broadcast_in_dim.2), channel_id=1, replica_groups={{576,592,608,624,512,528,544,560,704,720,736,752,640,656,672,688,832,84..., dimensions={0} | all-to-all | bytes 524288 | tf_op jit(solution)/shard_map/all_to_all | solution.py:19
  68.6 2.9 %factor.1 = (f32[64,896]{1,0:T(8,128)S(1)}, f32[64,64]{1,0:T(8,128)S(1)}, f32[16,1,128]{2,1,0:T(1,128)}) custom-call(f32[64,8,128]{2,1,0:T(8,128)S(1)} %all_to_all.22.whole_ref, f32[64,64]{1,0:T(8,128)S(1)} %get-tuple-element.11.left_ref), custom_call_target="tpu_custom_call" | custom-call | tf_op jit(solution)/shard_map/factor/pallas_call | solution.py:143
  71.5 6.5 %all-to-all-start.3 = ((f32[16,1,128]{2,1,0:T(1,128)}), f32[16,1,128]{2,1,0:T(1,128)S(1)}, u32[]{:S(2)}, u32[]{:S(2)}) async-start(f32[16,1,128]{2,1,0:T(1,128)} %get-tuple-element.12), calls=%async_computation.3 | async-start | bytes 16384 | tf_op jit(solution)/shard_map/all_to_all | solution.py:19
  77.9 0.0 copy-start.1
  77.9 0.9 %momentum.1 = f32[64,896]{1,0:T(8,128)} custom-call(f32[64,896]{1,0:T(8,128)S(1)} %get-tuple-element.13.right_ref, f32[64,64]{1,0:T(8,128)S(1)} %get-tuple-element.14.ortho_ref, f32[64,896]{1,0:T(8,128)S(1)} %convert_add_fusion.buffer_ref), custom_call_target="tpu_custom_call" | custom-call | tf_op jit(solution)/shard_map/momentum/pallas_call | solution.py:143
  78.9 3.8 %all-to-all-done.3.squares_ref = f32[16,1,128]{2,1,0:T(1,128)S(1)} async-done(((f32[16,1,128]{2,1,0:T(1,128)}), f32[16,1,128]{2,1,0:T(1,128)S(1)}, u32[]{:S(2)}, u32[]{:S(2)}) %all-to-all-start.3) | async-done | bytes 8224 | tf_op jit(solution)/shard_map/all_to_all | solution.py:19
  82.6 0.0 copy-done.1
  82.6 1.0 %weight.1 = (f32[64,896]{1,0:T(8,128)}, f32[64,896]{1,0:T(8,128)}) custom-call(f32[16,1,128]{2,1,0:T(1,128)S(1)} %all-to-all-done.3.squares_ref, f32[64,896]{1,0:T(8,128)S(1)} %get-tuple-element.13.right_ref, f32[64,64]{1,0:T(8,128)S(1)} %get-tuple-element.14.ortho_ref, f32[64,896]{1,0:T(8,128)S(1)} %copy-done.1), custom_call_target="tpu_custom_call" | custom-call | tf_op jit(solution)/shard_map/weight/pallas_call | solution.py:143
  (1 shorter events, 0.0 us)
Async XLA Ops:
  0.6 1.1 %copy-start = (f32[896,64]{0,1:T(8,128)S(1)}, f32[896,64]{0,1:T(8,128)}, u32[]{:S(2)}) copy-start(f32[896,64]{0,1:T(8,128)} %param.7) | copy-start | bytes 688132
  71.5 11.2 %all-to-all-start.3 = ((f32[16,1,128]{2,1,0:T(1,128)}), f32[16,1,128]{2,1,0:T(1,128)S(1)}, u32[]{:S(2)}, u32[]{:S(2)}) async-start(f32[16,1,128]{2,1,0:T(1,128)} %get-tuple-element.12), calls=%async_computation.3 | async-start | bytes 16384 | tf_op jit(solution)/shard_map/all_to_all | solution.py:19
  77.9 4.7 %copy-start.1 = (f32[64,896]{1,0:T(8,128)S(1)}, f32[64,896]{1,0:T(8,128)}, u32[]{:S(2)}) copy-start(f32[64,896]{1,0:T(8,128)} %weight_ref.1) | copy-start | bytes 688132

commit v10 on v8

--- a/solution.py
+++ b/solution.py
@@ -55,7 +55,11 @@
             for later in range(k + 1, 8):
                 entry = spread_row(columns[later][first], k)
                 for i in live:
-                    columns[later][i] = columns[later][i] - ratio[i] * entry
+                    if i == first and later == k + 1:
+                        step = (columns[k][i] * entry) * inverse
+                    else:
+                        step = ratio[i] * entry
+                    columns[later][i] = columns[later][i] - step
             if k < 7:
                 blocks[first] = blocks[first] - below * row
             for i in range(first + 1, count):
@@ -86,7 +90,14 @@
 
 
 def left_kernel(buffer_ref, basis_ref, copies_ref):
-    part = dot(buffer_ref[...], basis_ref[...], ((1,), (1,)))
+    buffer, basis = terms(buffer_ref[...], 3), terms(basis_ref[...], 3)
+    pairs = [(i, j) for i in range(3) for j in range(3) if i + j < 3]
+    part = dot(
+        jnp.concatenate([buffer[i] for i, _ in pairs], axis=1),
+        jnp.concatenate([basis[j] for _, j in pairs], axis=1),
+        ((1,), (1,)),
+        lax.Precision.DEFAULT,
+    )
     half = part.shape[0] // 2
     packed = jnp.concatenate([part[:half], part[half:]], axis=1)
     copies_ref[...] = jnp.broadcast_to(packed[None], copies_ref.shape)

time: 83.3 us -> 83.2 us (level)
  no operation moved by 1% of the time
where the time goes in v10:
time: 83.2 us; the launch traced here: 82.9 us
  blocking collectives  76.9 us (92%)
  Pallas kernels  4.19 us (5%)
  other arithmetic  1.14 us (1%)
    all_to_all x4, blocking collectives, exchange(): return lax.all_to_all(blocks, axis, 0, 0, axis_index_groups=[order(axis)])  76.9 us
    pallas_call x4, Pallas kernels, call(): pl.pallas_call(kernel, out_shape=[jax.ShapeDtypeStruct(shape, f32) for sh...  4.19 us

profile of v10, /device:TPU:1, one launch (start us, length us, event | category | flops | bytes accessed | tf_op | source)
XLA Modules:
  0.0 82.9 jit_solution(11580925939486964010)
XLA Ops:
  0.6 0.0 copy-start
  0.6 1.1 %convert_add_fusion.buffer_ref = f32[64,896]{1,0:T(8,128)S(1)} fusion(f32[64,896]{1,0:T(8,128)} %param.5, bf16[64,896]{1,0:T(8,128)(2,1)} %param.6), kind=kLoop, calls=%fused_computation | loop fusion | flops 114688 | bytes 573440 | tf_op jit(solution)/shard_map/add | solution.py:169
  1.7 0.0 copy-done
  1.7 0.4 left.1
  2.2 27.3 %all_to_all.20.parts_ref = f32[16,32,128]{2,1,0:T(8,128)S(1)} all-to-all(f32[16,32,128]{2,1,0:T(8,128)S(1)} %left.1), channel_id=1, replica_groups={{15,14,1,0,3,2,13,12,5,4,11,10,7,6,9,8},{31,30,17,16,19,18,29,28,21,20,..., dimensions={0} | all-to-all | bytes 524288 | tf_op jit(solution)/shard_map/all_to_all | solution.py:19
  29.5 0.5 products.1
  29.9 20.8 %all_to_all.21 = f32[64,8,128]{2,1,0:T(8,128)S(1)} all-to-all(f32[64,8,128]{2,1,0:T(8,128)S(1)} %get-tuple-element.11), channel_id=1, replica_groups={{576,592,608,624,512,528,544,560,704,720,736,752,640,656,672,688,832,84..., dimensions={0} | all-to-all | bytes 524288 | tf_op jit(solution)/shard_map/all_to_all | solution.py:19
  50.8 0.1 reduce_sum.9
  50.8 17.7 %all_to_all.22.whole_ref = f32[64,8,128]{2,1,0:T(8,128)S(1)} all-to-all(f32[64,8,128]{2,1,0:T(8,128)S(1)} %broadcast_in_dim.2), channel_id=1, replica_groups={{576,592,608,624,512,528,544,560,704,720,736,752,640,656,672,688,832,84..., dimensions={0} | all-to-all | bytes 524288 | tf_op jit(solution)/shard_map/all_to_all | solution.py:19
  68.6 0.0 copy-start.1
  68.6 2.2 %factor.1 = (f32[64,896]{1,0:T(8,128)S(1)}, f32[64,64]{1,0:T(8,128)S(1)}, f32[16,1,128]{2,1,0:T(1,128)S(1)}) custom-call(f32[64,8,128]{2,1,0:T(8,128)S(1)} %all_to_all.22.whole_ref, f32[64,64]{1,0:T(8,128)S(1)} %get-tuple-element.12.left_ref), custom_call_target="tpu_custom_call" | custom-call | tf_op jit(solution)/shard_map/factor/pallas_call | solution.py:155
  70.8 11.0 %all_to_all.23.squares_ref = f32[16,1,128]{2,1,0:T(1,128)S(1)} all-to-all(f32[16,1,128]{2,1,0:T(1,128)S(1)} %get-tuple-element.13), channel_id=1, replica_groups={{15,14,1,0,3,2,13,12,5,4,11,10,7,6,9,8},{31,30,17,16,19,18,29,28,21,20,..., dimensions={0} | all-to-all | bytes 16384 | tf_op jit(solution)/shard_map/all_to_all | solution.py:19
  81.8 0.0 copy-done.1
  81.8 1.1 %update.1 = (f32[64,896]{1,0:T(8,128)}, f32[64,896]{1,0:T(8,128)}, f32[64,896]{1,0:T(8,128)}) custom-call(f32[16,1,128]{2,1,0:T(1,128)S(1)} %all_to_all.23.squares_ref, f32[64,896]{1,0:T(8,128)S(1)} %get-tuple-element.14.right_ref, f32[64,64]{1,0:T(8,128)S(1)} %get-tuple-element.15.ortho_ref, f32[64,896]{1,0:T(8,128)S(1)} %convert_add_fusion.buffer_ref, ...), custom_call_target="tpu_custom_call" | custom-call | tf_op jit(solution)/shard_map/update/pallas_call | solution.py:155
  (1 shorter events, 0.0 us)
Async XLA Ops:
  0.6 1.1 %copy-start = (f32[896,64]{0,1:T(8,128)S(1)}, f32[896,64]{0,1:T(8,128)}, u32[]{:S(2)}) copy-start(f32[896,64]{0,1:T(8,128)} %param.7) | copy-start | bytes 688132
  68.6 13.3 %copy-start.1 = (f32[64,896]{1,0:T(8,128)S(1)}, f32[64,896]{1,0:T(8,128)}, u32[]{:S(2)}) copy-start(f32[64,896]{1,0:T(8,128)} %weight_ref.1) | copy-start | bytes 688132

commit v11 on v10

--- a/solution.py
+++ b/solution.py
@@ -26,7 +26,8 @@
         others = sorted(range(planes - 1), key=lambda z: (min(z, planes - z), -z))
         return [2 * z + core for z in [planes - 1] + others for core in (1, 0)]
     side = math.isqrt(count)
-    turned = [(i + 4) % side for i in range(side)]
+    middle = side // 2
+    turned = sorted(range(side), key=lambda i: (abs(i - middle), i))
     return [side * y + x for y in turned for x in turned]
 
 

time: 83.2 us -> 83.5 us (level)
  no operation moved by 1% of the time
where the time goes in v11:
time: 83.5 us; the launch traced here: 83.2 us
  blocking collectives  77.2 us (92%)
  Pallas kernels  4.19 us (5%)
  other arithmetic  1.14 us (1%)
    all_to_all x4, blocking collectives, exchange(): return lax.all_to_all(blocks, axis, 0, 0, axis_index_groups=[order(axis)])  77.2 us
    pallas_call x4, Pallas kernels, call(): pl.pallas_call(kernel, out_shape=[jax.ShapeDtypeStruct(shape, f32) for sh...  4.19 us

profile of v11, /device:TPU:1, one launch (start us, length us, event | category | flops | bytes accessed | tf_op | source)
XLA Modules:
  0.0 83.2 jit_solution(7552576770382881764)
XLA Ops:
  0.6 0.0 copy-start
  0.6 1.1 %convert_add_fusion.buffer_ref = f32[64,896]{1,0:T(8,128)S(1)} fusion(f32[64,896]{1,0:T(8,128)} %param.5, bf16[64,896]{1,0:T(8,128)(2,1)} %param.6), kind=kLoop, calls=%fused_computation | loop fusion | flops 114688 | bytes 573440 | tf_op jit(solution)/shard_map/add | solution.py:170
  1.7 0.0 copy-done
  1.7 0.4 left.1
  2.2 27.3 %all_to_all.20.parts_ref = f32[16,32,128]{2,1,0:T(8,128)S(1)} all-to-all(f32[16,32,128]{2,1,0:T(8,128)S(1)} %left.1), channel_id=1, replica_groups={{15,14,1,0,3,2,13,12,5,4,11,10,7,6,9,8},{31,30,17,16,19,18,29,28,21,20,..., dimensions={0} | all-to-all | bytes 524288 | tf_op jit(solution)/shard_map/all_to_all | solution.py:19
  29.5 0.5 products.1
  29.9 21.1 %all_to_all.21 = f32[64,8,128]{2,1,0:T(8,128)S(1)} all-to-all(f32[64,8,128]{2,1,0:T(8,128)S(1)} %get-tuple-element.11), channel_id=1, replica_groups={{576,560,592,544,608,528,624,512,448,432,464,416,480,400,496,384,704,68..., dimensions={0} | all-to-all | bytes 524288 | tf_op jit(solution)/shard_map/all_to_all | solution.py:19
  51.0 0.1 reduce_sum.9
  51.1 18.4 %all_to_all.22.whole_ref = f32[64,8,128]{2,1,0:T(8,128)S(1)} all-to-all(f32[64,8,128]{2,1,0:T(8,128)S(1)} %broadcast_in_dim.2), channel_id=1, replica_groups={{576,560,592,544,608,528,624,512,448,432,464,416,480,400,496,384,704,68..., dimensions={0} | all-to-all | bytes 524288 | tf_op jit(solution)/shard_map/all_to_all | solution.py:19
  69.6 0.0 copy-start.1
  69.6 2.2 %factor.1 = (f32[64,896]{1,0:T(8,128)S(1)}, f32[64,64]{1,0:T(8,128)S(1)}, f32[16,1,128]{2,1,0:T(1,128)S(1)}) custom-call(f32[64,8,128]{2,1,0:T(8,128)S(1)} %all_to_all.22.whole_ref, f32[64,64]{1,0:T(8,128)S(1)} %get-tuple-element.12.left_ref), custom_call_target="tpu_custom_call" | custom-call | tf_op jit(solution)/shard_map/factor/pallas_call | solution.py:156
  71.8 10.3 %all_to_all.23.squares_ref = f32[16,1,128]{2,1,0:T(1,128)S(1)} all-to-all(f32[16,1,128]{2,1,0:T(1,128)S(1)} %get-tuple-element.13), channel_id=1, replica_groups={{15,14,1,0,3,2,13,12,5,4,11,10,7,6,9,8},{31,30,17,16,19,18,29,28,21,20,..., dimensions={0} | all-to-all | bytes 16384 | tf_op jit(solution)/shard_map/all_to_all | solution.py:19
  82.1 0.0 copy-done.1
  82.1 1.1 %update.1 = (f32[64,896]{1,0:T(8,128)}, f32[64,896]{1,0:T(8,128)}, f32[64,896]{1,0:T(8,128)}) custom-call(f32[16,1,128]{2,1,0:T(1,128)S(1)} %all_to_all.23.squares_ref, f32[64,896]{1,0:T(8,128)S(1)} %get-tuple-element.14.right_ref, f32[64,64]{1,0:T(8,128)S(1)} %get-tuple-element.15.ortho_ref, f32[64,896]{1,0:T(8,128)S(1)} %convert_add_fusion.buffer_ref, ...), custom_call_target="tpu_custom_call" | custom-call | tf_op jit(solution)/shard_map/update/pallas_call | solution.py:156
  (1 shorter events, 0.0 us)
Async XLA Ops:
  0.6 1.1 %copy-start = (f32[896,64]{0,1:T(8,128)S(1)}, f32[896,64]{0,1:T(8,128)}, u32[]{:S(2)}) copy-start(f32[896,64]{0,1:T(8,128)} %param.7) | copy-start | bytes 688132
  69.6 12.5 %copy-start.1 = (f32[64,896]{1,0:T(8,128)S(1)}, f32[64,896]{1,0:T(8,128)}, u32[]{:S(2)}) copy-start(f32[64,896]{1,0:T(8,128)} %weight_ref.1) | copy-start | bytes 688132
